TPU v7x, 256 devices: a whole 4x4x8 slice. The times are simulated.
256 devices in a mesh: band: 32 (over z, x_lo, core), slab: 8 (over x_hi, y).
Axes of the slice: x: 4 (x_hi: 2, x_lo: 2; x = x_hi * 2 + x_lo), y: 4, z: 8, core: 2. Of those that a mesh axis runs over, the one named last changes fastest.
Arguments:
- orbitals: float32 [128, 96, 4608], P('band', 'slab'), may hold values from -3 to 3
- owner: int32 [2], replicated, may hold values from 0 to 31
- picks: int32 [2, 2], replicated, may hold values from 0 to 3
Outputs:
- exchange_field: float32 [128, 96, 4608], P('band', 'slab')
- transposed: float32 [2, 2, 96, 4608], P(None, None, 'slab')
Inputs may be any that keep to these rules, and one draw needn't show every extreme that they name: owner names a band group and picks positions within it; the two picks of a step may coincide.
All inputs are finite; a program needn't handle non-finite values.
Results may differ from a plain program's by a relative error of at most 0.0001.
Values sent between devices are 32-bit elements; how exact they have to be, the bound alone decides.
No kernel may reach another device: no remote copies, remote signals or barrier semaphores. Data moves between devices by JAX's collectives and lax.ppermute only.
A program may use at most 128 MiB of HBM per device.

v0:
```python
import functools
import math

import jax
import jax.numpy as jnp
import ml_dtypes
import numpy as np
from jax import lax
from jax.experimental import pallas as pl
from jax.experimental.pallas import tpu as pltpu
from jax.sharding import Mesh, PartitionSpec as P

NX = 48
NY = 96
NZ = 96
BLOC = 4
STEPS = 2
SLABS = 8
PLANES = NZ // SLABS
POINTS = NY * NX
ROWS = BLOC * PLANES
PAIR = 2 * PLANES
BLOCKS = 12
INNER = 8
LANES = INNER * NX
HALF = LANES // 2
COLUMNS = 3 * LANES

length_first = 41.05
length_side = 41.05
length_last = 20.525
omega_screen = 0.106


def swap(x, axis, bit):
    size = lax.axis_size(axis)
    return lax.ppermute(x, axis, [(i, i ^ bit) for i in range(size)])


def split_sum(x, axis, bit):
    upper = (lax.axis_index(axis) & bit) != 0
    middle = x.shape[-1] // 2
    first, second = x[..., :middle], x[..., middle:]
    kept = jnp.where(upper, second, first)
    other = jnp.where(upper, first, second)
    return kept + swap(other, axis, bit)


def join(x, axis, bit):
    upper = (lax.axis_index(axis) & bit) != 0
    other = swap(x, axis, bit)
    return jnp.concatenate([jnp.where(upper, other, x), jnp.where(upper, x, other)], axis=-1)


def sum_over_bands(x):
    core = lax.axis_index("c")
    kept = jnp.where(core == 0, x[0], x[1])
    other = jnp.where(core == 0, x[1], x[0])
    part = kept + swap(other, "c", 1)
    part = split_sum(part, "z", 1)
    part = split_sum(part, "xl", 1)
    part = part + swap(part, "z", 2)
    part = part + swap(part, "z", 4)
    part = join(part, "xl", 1)
    part = join(part, "z", 1)
    other = swap(part, "c", 1)
    return jnp.stack([jnp.where(core == 0, part, other), jnp.where(core == 0, other, part)])


def frequency(counter, length):
    return jnp.where(counter <= length // 2, counter, counter - length).astype(jnp.float32)


def coulomb_kernel(freq_z, freq_y, freq_x):
    squared = (
        (2.0 * math.pi / length_first * freq_z) ** 2
        + (2.0 * math.pi / length_side * freq_y) ** 2
        + (2.0 * math.pi / length_last * freq_x) ** 2
    )
    safe = jnp.where(squared > 0, squared, 1.0)
    screened = -4.0 * math.pi * jnp.expm1(-squared / (4.0 * omega_screen**2)) / safe
    return jnp.where(squared > 0, screened, math.pi / omega_screen**2)


def kernel_columns(xh, y):
    kz = (jnp.arange(SLABS)[:, None] * PLANES + jnp.arange(PLANES)[None, :]).reshape(NZ, 1)
    lane = jnp.arange(3 * HALF)
    kb = 3 * y + lane // HALF
    kk = 4 * xh + lane % HALF // NX
    values = coulomb_kernel(
        frequency(kz, NZ), frequency(kb + BLOCKS * kk, NY)[None, :], frequency(lane % NX, NX)[None, :]
    ) * (1.0 / (NX * NY * NZ))
    values = values.reshape(SLABS, 1, PLANES, 3, 1, HALF)
    return jnp.broadcast_to(values, (SLABS, 2, PLANES, 3, 2, HALF)).reshape(2 * NZ, COLUMNS)


def split_table(table):
    high = table.astype(ml_dtypes.bfloat16)
    low = (table - high.astype(np.float64)).astype(ml_dtypes.bfloat16)
    return high, low


@functools.cache
def tables():
    inner, x = np.divmod(np.arange(LANES), NX)
    angle = -2.0 * np.pi * (
        (inner[:, None] * inner[None, :] % INNER) / INNER + (x[:, None] * x[None, :] % NX) / NX
    )
    real, imag = np.cos(angle), np.sin(angle)
    forward = np.zeros((2, LANES, 2, 2, HALF))
    inverse = np.zeros((2, 2, HALF, 2, LANES))
    for half in range(2):
        part = slice(half * HALF, (half + 1) * HALF)
        forward[0, :, half, 0], forward[1, :, half, 0] = real[:, part], -imag[:, part]
        forward[0, :, half, 1], forward[1, :, half, 1] = imag[:, part], real[:, part]
        inverse[half, 0, :, 0], inverse[half, 1, :, 0] = real[part], imag[part]
        inverse[half, 0, :, 1], inverse[half, 1, :, 1] = -imag[part], real[part]
    forward = split_table(forward.reshape(2 * LANES, 2 * LANES))
    inverse = split_table(inverse.reshape(2 * LANES, 2 * LANES))
    turn = -2.0 * np.pi / NY * (np.arange(BLOCKS)[:, None] * inner[None, :] % NY)
    twiddle = np.cos(turn).astype(np.float32), np.sin(turn).astype(np.float32)
    slab, rest = np.divmod(np.arange(2 * NZ), PAIR)
    band, plane = np.divmod(rest, PLANES)
    z = slab * PLANES + plane
    same = band[:, None] == band[None, :]
    angle = 2.0 * np.pi / NZ * (z[:, None] * z[None, :] % NZ)
    stacked = np.concatenate([np.where(same, np.cos(angle), 0), np.where(same, np.sin(angle), 0)])
    high, low = split_table(stacked)
    along_z = np.concatenate([high, high, low], axis=1)
    return forward, inverse, twiddle, along_z


def split(x):
    high = x.astype(jnp.bfloat16)
    return high, (x - high.astype(jnp.float32)).astype(jnp.bfloat16)


def dot(a, b):
    return lax.dot_general(a, b, (((1,), (0,)), ((), ())), preferred_element_type=jnp.float32)


def dft12(values, sign):
    def turn(value):
        re, im = value
        return (-im, re) if sign > 0 else (im, -re)

    def add(a, b):
        return a[0] + b[0], a[1] + b[1]

    def sub(a, b):
        return a[0] - b[0], a[1] - b[1]

    quarter = []
    for n1 in range(3):
        a = [values[(4 * n1 + 3 * n2) % 12] for n2 in range(4)]
        even, odd = add(a[0], a[2]), add(a[1], a[3])
        left, right = sub(a[0], a[2]), turn(sub(a[1], a[3]))
        quarter.append([add(even, odd), add(left, right), sub(even, odd), sub(left, right)])
    result = [None] * 12
    for k4 in range(4):
        b = [quarter[n1][k4] for n1 in range(3)]
        total = add(b[1], b[2])
        difference = sub(b[1], b[2])
        middle = (b[0][0] - 0.5 * total[0], b[0][1] - 0.5 * total[1])
        scale = math.sqrt(0.75)
        side = turn((scale * difference[0], scale * difference[1]))
        for k3, value in enumerate((add(b[0], total), add(middle, side), sub(middle, side))):
            where = next(k for k in range(12) if k % 3 == k3 and k % 4 == k4)
            result[where] = value
    return result


def forward_kernel(orbital_ref, chosen_ref, cos_ref, sin_ref, high_ref, low_ref, out_ref, field, field_high, field_low):
    steps = chosen_ref.shape[0]
    for step in range(steps):

        def tile(index, carry):
            for group in range(2):
                for part in range(3):
                    rows = pl.ds(pl.multiple_of(group * PAIR + index * 8, 8), 8)
                    own = pl.ds(pl.multiple_of(index * 8, 8), 8)
                    values = []
                    for block in range(BLOCKS):
                        lanes = pl.ds(block * LANES + part * 128, 128)
                        orbital = orbital_ref[rows, lanes]
                        values.append(
                            (orbital * chosen_ref[step, 0, own, lanes], orbital * chosen_ref[step, 1, own, lanes])
                        )
                    values = dft12(values, -1)
                    for kb, (re, im) in enumerate(values):
                        cosine = cos_ref[kb : kb + 1, part * 128 : part * 128 + 128]
                        sine = sin_ref[kb : kb + 1, part * 128 : part * 128 + 128]
                        to = pl.ds(pl.multiple_of(kb * ROWS + group * PAIR + index * 8, 8), 8)
                        field[to, pl.ds(part * 128, 128)] = re * cosine - im * sine
                        field[to, pl.ds(LANES + part * 128, 128)] = re * sine + im * cosine
            return carry

        lax.fori_loop(0, PAIR // 8, tile, 0)
        field_high[...], field_low[...] = split(field[...])
        for piece in range(3):
            lanes = pl.ds(piece * 256, 256)
            high = high_ref[:, lanes]
            result = dot(field_high[...], high) + dot(field_low[...], high) + dot(field_high[...], low_ref[:, lanes])
            for part in range(2):
                half, offset = divmod(2 * piece + part, 3)
                for kb in range(BLOCKS):
                    column, turn = divmod(kb, 3)
                    out_ref[
                        half * 4 + column, pl.ds(step * ROWS, ROWS), pl.ds(turn * LANES + offset * 128, 128)
                    ] = result[kb * ROWS : kb * ROWS + ROWS, part * 128 : part * 128 + 128]


def middle_kernel(value_ref, kernel_ref, table_ref, out_ref):
    rows = value_ref.shape[1]
    imaginary = lax.broadcasted_iota(jnp.int32, (2 * NZ, LANES), 1) >= HALF

    def swapped(x):
        return jnp.concatenate([x[:, HALF:], x[:, :HALF]], axis=1)

    def transform(x, sign):
        high, low = split(x)
        both = dot(table_ref[...], jnp.concatenate([high, low, high], axis=0))
        cosine, sine = both[: 2 * NZ], swapped(both[2 * NZ :])
        return cosine + jnp.where(imaginary, -sign * sine, sign * sine)

    for group in range(rows // PAIR):
        own = slice(group * PAIR, group * PAIR + PAIR)
        for turn in range(3):
            lanes = slice(turn * LANES, turn * LANES + LANES)
            x = jnp.concatenate([value_ref[slab, own, lanes] for slab in range(SLABS)], axis=0)
            x = transform(x, 1.0) * kernel_ref[:, lanes]
            x = transform(x, -1.0)
            for slab in range(SLABS):
                out_ref[slab, own, lanes] = x[slab * PAIR : slab * PAIR + PAIR]


def inverse_kernel(
    value_ref, orbital_ref, chosen_ref, cos_ref, sin_ref, high_ref, low_ref, applied_ref, summed_ref, field_high, field_low, field, totals
):
    steps = chosen_ref.shape[0]
    for step in range(steps):
        for kb in range(BLOCKS):
            column, turn = divmod(kb, 3)
            for half in range(2):
                x = value_ref[half * 4 + column, pl.ds(step * ROWS, ROWS), pl.ds(turn * LANES, LANES)]
                high, low = split(x)
                field_high[kb * ROWS : kb * ROWS + ROWS, half * LANES : half * LANES + LANES] = high
                field_low[kb * ROWS : kb * ROWS + ROWS, half * LANES : half * LANES + LANES] = low
        for piece in range(3):
            lanes = pl.ds(piece * 256, 256)
            high = high_ref[:, lanes]
            field[:, lanes] = (
                dot(field_high[...], high) + dot(field_low[...], high) + dot(field_high[...], low_ref[:, lanes])
            )

        def tile(index, carry):
            own = pl.ds(pl.multiple_of(index * 8, 8), 8)
            for part in range(3):
                for group in range(2):
                    rows = pl.ds(pl.multiple_of(group * PAIR + index * 8, 8), 8)
                    values = []
                    for kb in range(BLOCKS):
                        cosine = cos_ref[kb : kb + 1, part * 128 : part * 128 + 128]
                        sine = sin_ref[kb : kb + 1, part * 128 : part * 128 + 128]
                        at = pl.ds(pl.multiple_of(kb * ROWS + group * PAIR + index * 8, 8), 8)
                        re = field[at, pl.ds(part * 128, 128)]
                        im = field[at, pl.ds(LANES + part * 128, 128)]
                        values.append((re * cosine + im * sine, im * cosine - re * sine))
                    values = dft12(values, 1)
                    for block, (first, second) in enumerate(values):
                        lanes = pl.ds(block * LANES + part * 128, 128)
                        orbital = orbital_ref[rows, lanes]
                        applied = first * chosen_ref[step, 0, own, lanes] + second * chosen_ref[step, 1, own, lanes]
                        if step == 0:
                            applied_ref[rows, lanes] = applied
                        else:
                            applied_ref[rows, lanes] += applied
                        if group == 0:
                            totals[0, own, lanes] = first * orbital
                            totals[1, own, lanes] = second * orbital
                        else:
                            totals[0, own, lanes] += first * orbital
                            totals[1, own, lanes] += second * orbital
            return carry

        lax.fori_loop(0, PAIR // 8, tile, 0)
        for block in range(BLOCKS):
            lanes = pl.ds(block * LANES, LANES)
            first = totals[0, :PLANES, lanes] + totals[0, PLANES:, lanes]
            second = totals[1, :PLANES, lanes] + totals[1, PLANES:, lanes]
            summed_ref[step, :, lanes] = jnp.concatenate([first, second], axis=0)


PARAMS = dict(compiler_params=pltpu.CompilerParams(vmem_limit_bytes=48 * 1024 * 1024))
VMEM = pl.BlockSpec(memory_space=pltpu.VMEM)


def cost(operations, size):
    return pl.CostEstimate(flops=operations, bytes_accessed=size, transcendentals=0)


def to_columns(orbitals, chosen):
    steps = chosen.shape[0]
    forward, _, twiddle, _ = tables()
    tall = BLOCKS * ROWS
    return pl.pallas_call(
        forward_kernel,
        out_shape=jax.ShapeDtypeStruct((SLABS, steps * ROWS, COLUMNS), jnp.float32),
        in_specs=[VMEM] * 6,
        out_specs=VMEM,
        scratch_shapes=[
            pltpu.VMEM((tall, 2 * LANES), jnp.float32),
            pltpu.VMEM((tall, 2 * LANES), jnp.bfloat16),
            pltpu.VMEM((tall, 2 * LANES), jnp.bfloat16),
        ],
        cost_estimate=cost(steps * 6 * tall * (2 * LANES) ** 2, steps * 4_000_000),
        **PARAMS,
    )(orbitals, chosen, *twiddle, *forward)


def screened(values, kernel):
    _, _, _, along_z = tables()
    return pl.pallas_call(
        middle_kernel,
        out_shape=jax.ShapeDtypeStruct(values.shape, jnp.float32),
        in_specs=[VMEM] * 3,
        out_specs=VMEM,
        cost_estimate=cost(values.shape[1] // PAIR * 4 * 4 * NZ * 6 * NZ * COLUMNS, 8 * values.size),
        **PARAMS,
    )(values, kernel, along_z)


def from_columns(values, orbitals, chosen):
    steps = chosen.shape[0]
    _, inverse, twiddle, _ = tables()
    tall = BLOCKS * ROWS
    return pl.pallas_call(
        inverse_kernel,
        out_shape=(
            jax.ShapeDtypeStruct((ROWS, POINTS), jnp.float32),
            jax.ShapeDtypeStruct((steps, PAIR, POINTS), jnp.float32),
        ),
        in_specs=[VMEM] * 7,
        out_specs=(VMEM, VMEM),
        scratch_shapes=[
            pltpu.VMEM((tall, 2 * LANES), jnp.bfloat16),
            pltpu.VMEM((tall, 2 * LANES), jnp.bfloat16),
            pltpu.VMEM((tall, 2 * LANES), jnp.float32),
            pltpu.VMEM((2, PAIR, POINTS), jnp.float32),
        ],
        cost_estimate=cost(steps * 6 * tall * (2 * LANES) ** 2, steps * 4_000_000),
        **PARAMS,
    )(values, orbitals, chosen, *twiddle, *inverse)


def per_device(orbitals, owner, picks):
    group = (lax.axis_index("z") * 2 + lax.axis_index("xl")) * 2 + lax.axis_index("c")
    picked = jnp.take(orbitals, picks.reshape(-1), axis=0).reshape(STEPS, 2, PLANES, POINTS)
    mine = (owner == group)[:, None, None, None]
    picked = jnp.where(mine, picked, 0.0).reshape(STEPS, PAIR, POINTS)
    chosen = sum_over_bands(picked).reshape(STEPS, 2, PLANES, POINTS)
    chosen = jnp.concatenate([chosen, chosen], axis=2)
    kernel = kernel_columns(lax.axis_index("xh"), lax.axis_index("y"))
    flat = orbitals.reshape(ROWS, POINTS)
    columns = to_columns(flat, chosen)
    columns = lax.all_to_all(columns, ("xh", "y"), split_axis=0, concat_axis=0, tiled=True)
    columns = screened(columns, kernel)
    columns = lax.all_to_all(columns, ("xh", "y"), split_axis=0, concat_axis=0, tiled=True)
    applied, local_sum = from_columns(columns, flat, chosen)
    transposed = sum_over_bands(local_sum).reshape(STEPS, 2, PLANES, POINTS)
    return applied.reshape(BLOC, PLANES, POINTS), transposed


def solution(mesh):
    fine = Mesh(mesh.devices.reshape(8, 2, 2, 2, 4), ("z", "xl", "c", "xh", "y"))
    band, slab = ("z", "xl", "c"), ("xh", "y")
    in_specs = (P(band, slab, None), P(), P())
    out_specs = (P(band, slab, None), P(None, None, slab, None))
    return jax.shard_map(
        per_device, mesh=fine, in_specs=in_specs, out_specs=out_specs, check_vma=False
    )
```

profile of v0, /device:TPU:1, one launch (start us, length us, event | category | flops | bytes accessed | tf_op | source)
XLA Modules:
  0.0 229.7 jit_solution(5530515580444592926)
XLA Ops:
  0.6 0.8 reshape.205
  1.4 0.7 compare_and_fusion
  2.1 3.1 %gather_fusion = f32[4,12,4608]{2,0,1:T(4,128)S(1)} fusion(f32[4,12,4608]{2,0,1:T(4,128)} %param.10, s32[1024]{0:T(1024)S(1)} %pad_clamp_fusion), kind=kCustom, calls=%fused_computation | custom fusion | bytes 1769488 | tf_op jit(solution)/shard_map/jit(_take)/gather | solution.py:358
  5.2 0.3 copy.21
  5.5 0.3 copy-done.9
  6.1 3.3 %collective-permute-start = (f32[24,4608]{1,0:T(8,128)S(1)}, f32[24,4608]{1,0:T(8,128)S(1)}, u32[]{:S(2)}, u32[]{:S(2)}) collective-permute-start(f32[24,4608]{1,0:T(8,128)S(1)} %select_n.234), channel_id=1, source_target_pairs={{0,8},{8,0},{1,9},{9,1},{2,10},{10,2},{3,11},{11,3},{4,12},{12,4},... | collective-permute-start | bytes 1327112 | tf_op jit(solution)/shard_map/ppermute | solution.py:37
  9.5 1.4 collective-permute-done
  11.1 6.6 %collective-permute-done.1 = f32[24,2304]{1,0:T(8,128)S(1)} collective-permute-done((f32[24,2304]{1,0:T(8,128)S(1)}, f32[24,2304]{1,0:T(8,128)S(1)}, u32[]{:S(2)}, u32[]{:S(2)}) %collective-permute-start.1) | collective-permute-done | bytes 221216 | tf_op jit(solution)/shard_map/ppermute | solution.py:37
  17.9 3.6 %collective-permute-done.2 = f32[24,1152]{1,0:T(8,128)S(1)} collective-permute-done((f32[24,1152]{1,0:T(8,128)S(1)}, f32[24,1152]{1,0:T(8,128)S(1)}, u32[]{:S(2)}, u32[]{:S(2)}) %collective-permute-start.2) | collective-permute-done | bytes 110624 | tf_op jit(solution)/shard_map/ppermute | solution.py:37
  21.5 1.7 collective-permute-start.3
  23.2 4.1 %collective-permute-done.3 = f32[24,1152]{1,0:T(8,128)S(1)} collective-permute-done((f32[24,1152]{1,0:T(8,128)S(1)}, f32[24,1152]{1,0:T(8,128)S(1)}, u32[]{:S(2)}, u32[]{:S(2)}) %collective-permute-start.3) | collective-permute-done | bytes 110624 | tf_op jit(solution)/shard_map/ppermute | solution.py:37
  27.3 5.3 %collective-permute-start.4 = (f32[24,1152]{1,0:T(8,128)S(1)}, f32[24,1152]{1,0:T(8,128)S(1)}, u32[]{:S(2)}, u32[]{:S(2)}) collective-permute-start(f32[24,1152]{1,0:T(8,128)S(1)} %add.185), channel_id=1, source_target_pairs={{0,128},{32,160},{64,192},{96,224},{128,0},{160,32},{192,64},{224,... | collective-permute-start | bytes 331784 | tf_op jit(solution)/shard_map/ppermute | solution.py:37
  32.5 2.4 %collective-permute-done.4 = f32[24,1152]{1,0:T(8,128)S(1)} collective-permute-done((f32[24,1152]{1,0:T(8,128)S(1)}, f32[24,1152]{1,0:T(8,128)S(1)}, u32[]{:S(2)}, u32[]{:S(2)}) %collective-permute-start.4) | collective-permute-done | bytes 110624 | tf_op jit(solution)/shard_map/ppermute | solution.py:37
  34.9 1.3 collective-permute-start.5
  36.2 2.7 %collective-permute-done.5 = f32[24,1152]{1,0:T(8,128)S(1)} collective-permute-done((f32[24,1152]{1,0:T(8,128)S(1)}, f32[24,1152]{1,0:T(8,128)S(1)}, u32[]{:S(2)}, u32[]{:S(2)}) %collective-permute-start.5) | collective-permute-done | bytes 110624 | tf_op jit(solution)/shard_map/ppermute | solution.py:37
  39.0 0.4 collective-permute-start.6
  39.4 4.8 %collective-permute-done.6 = f32[24,2304]{1,0:T(8,128)S(1)} collective-permute-done((f32[24,2304]{1,0:T(8,128)S(1)}, f32[24,2304]{1,0:T(8,128)S(1)}, u32[]{:S(2)}, u32[]{:S(2)}) %collective-permute-start.6) | collective-permute-done | bytes 221216 | tf_op jit(solution)/shard_map/ppermute | solution.py:37
  44.2 6.6 %collective-permute-start.7 = (f32[24,4608]{1,0:T(8,128)S(1)}, f32[24,4608]{1,0:T(8,128)S(1)}, u32[]{:S(2)}, u32[]{:S(2)}) collective-permute-start(f32[24,4608]{1,0:T(8,128)S(1)} %pad_maximum_fusion.1), channel_id=1, source_target_pairs={{0,8},{8,0},{1,9},{9,1},{2,10},{10,2},{3,11},{11,3},{4,12},{12,4},... | collective-permute-start | bytes 1327112 | tf_op jit(solution)/shard_map/ppermute | solution.py:37
  50.8 0.3 copy.17
  51.2 1.0 collective-permute-done.7
  52.3 0.9 stack.19
  53.2 1.6 maximum_maximum_fusion.chosen_ref
  54.8 0.4 copy-done.4
  55.1 8.7 %shard_map.113 = f32[8,96,1152]{2,1,0:T(8,128)} custom-call(f32[48,4608]{1,0:T(8,128)S(1)} %reshape.204.orbital_ref, f32[2,2,24,4608]{3,2,1,0:T(8,128)S(1)} %maximum_maximum_fusion.chosen_ref, f32[12,384]{1,0:T(8,128)S(1)} %copy-done.6, f32[12,384]{1,0:T(8,128)S(1)} %copy-done.7, bf16[768,768]{1,0:T(8,128)(2,1)S(1)} %copy-done.3, bf16[768,768]{1,0:T(8,128)(2,1)S(1)} %copy-done.4), custom_call_target="tpu_custom_call" | custom-call | flops 4076863488 | bytes 8000000 | tf_op jit(solution)/shard_map/pallas_call | solution.py:306
  63.8 6.7 %all-to-all-start = ((f32[8,96,1152]{2,1,0:T(8,128)}), f32[8,96,1152]{2,1,0:T(8,128)}, u32[]{:S(2)}, u32[]{:S(2)}) async-start(f32[8,96,1152]{2,1,0:T(8,128)} %shard_map.113), calls=%async_computation | async-start | bytes 7077888 | tf_op jit(solution)/shard_map/all_to_all | solution.py:366
  70.6 0.5 fusion.1
  71.1 1.3 broadcast_in_dim.45
  72.5 2.3 reshape.206.kernel_ref
  74.7 37.5 %all-to-all-done.value_ref = f32[8,96,1152]{2,1,0:T(8,128)} async-done(((f32[8,96,1152]{2,1,0:T(8,128)}), f32[8,96,1152]{2,1,0:T(8,128)}, u32[]{:S(2)}, u32[]{:S(2)}) %all-to-all-start) | async-done | bytes 3538976 | tf_op jit(solution)/shard_map/all_to_all | solution.py:366
  112.2 11.9 %shard_map.114 = f32[8,96,1152]{2,1,0:T(8,128)S(1)} custom-call(f32[8,96,1152]{2,1,0:T(8,128)} %all-to-all-done.value_ref, f32[192,1152]{1,0:T(8,128)S(1)} %reshape.206.kernel_ref, bf16[384,576]{1,0:T(8,128)(2,1)S(1)} %copy-done.5), custom_call_target="tpu_custom_call" | custom-call | flops 4076863488 | bytes 7077888 | tf_op jit(solution)/shard_map/pallas_call | solution.py:323
  124.2 48.1 %all_to_all.10.value_ref = f32[8,96,1152]{2,1,0:T(8,128)} all-to-all(f32[8,96,1152]{2,1,0:T(8,128)S(1)} %shard_map.114), channel_id=1, replica_groups=mesh['z'=8,'xl'=2,'c'=2,'xh'=2,'y'=4] {'xh','y'}, dimensions={0} | all-to-all | bytes 7077888 | tf_op jit(solution)/shard_map/all_to_all | solution.py:368
  172.2 9.9 %shard_map.115 = (f32[48,4608]{1,0:T(8,128)S(1)}, f32[2,24,4608]{2,1,0:T(8,128)S(1)}) custom-call(f32[8,96,1152]{2,1,0:T(8,128)} %all_to_all.10.value_ref, f32[48,4608]{1,0:T(8,128)S(1)} %reshape.204.orbital_ref, f32[2,2,24,4608]{3,2,1,0:T(8,128)} %copy-done, f32[12,384]{1,0:T(8,128)S(1)} %copy-done.6, f32[12,384]{1,0:T(8,128)S(1)} %copy-done.7, ...), custom_call_target="tpu_custom_call" | custom-call | flops 4076863488 | bytes 8000000 | tf_op jit(solution)/shard_map/pallas_call | solution.py:337
  182.2 2.1 collective-permute-start.8
  184.2 1.4 collective-permute-done.8
  185.9 6.6 %collective-permute-done.9 = f32[24,2304]{1,0:T(8,128)S(1)} collective-permute-done((f32[24,2304]{1,0:T(8,128)S(1)}, f32[24,2304]{1,0:T(8,128)S(1)}, u32[]{:S(2)}, u32[]{:S(2)}) %collective-permute-start.9) | collective-permute-done | bytes 221216 | tf_op jit(solution)/shard_map/ppermute | solution.py:37
  192.6 0.9 collective-permute-start.10
  193.4 2.8 %collective-permute-done.10 = f32[24,1152]{1,0:T(8,128)S(1)} collective-permute-done((f32[24,1152]{1,0:T(8,128)S(1)}, f32[24,1152]{1,0:T(8,128)S(1)}, u32[]{:S(2)}, u32[]{:S(2)}) %collective-permute-start.10) | collective-permute-done | bytes 110624 | tf_op jit(solution)/shard_map/ppermute | solution.py:37
  196.3 1.5 collective-permute-start.11
  197.8 4.3 %collective-permute-done.11 = f32[24,1152]{1,0:T(8,128)S(1)} collective-permute-done((f32[24,1152]{1,0:T(8,128)S(1)}, f32[24,1152]{1,0:T(8,128)S(1)}, u32[]{:S(2)}, u32[]{:S(2)}) %collective-permute-start.11) | collective-permute-done | bytes 110624 | tf_op jit(solution)/shard_map/ppermute | solution.py:37
  202.1 5.2 %collective-permute-start.12 = (f32[24,1152]{1,0:T(8,128)S(1)}, f32[24,1152]{1,0:T(8,128)S(1)}, u32[]{:S(2)}, u32[]{:S(2)}) collective-permute-start(f32[24,1152]{1,0:T(8,128)S(1)} %add.205), channel_id=1, source_target_pairs={{0,128},{32,160},{64,192},{96,224},{128,0},{160,32},{192,64},{224,... | collective-permute-start | bytes 331784 | tf_op jit(solution)/shard_map/ppermute | solution.py:37
  207.3 2.5 %collective-permute-done.12 = f32[24,1152]{1,0:T(8,128)S(1)} collective-permute-done((f32[24,1152]{1,0:T(8,128)S(1)}, f32[24,1152]{1,0:T(8,128)S(1)}, u32[]{:S(2)}, u32[]{:S(2)}) %collective-permute-start.12) | collective-permute-done | bytes 110624 | tf_op jit(solution)/shard_map/ppermute | solution.py:37
  209.8 0.9 collective-permute-start.13
  210.7 3.1 %collective-permute-done.13 = f32[24,1152]{1,0:T(8,128)S(1)} collective-permute-done((f32[24,1152]{1,0:T(8,128)S(1)}, f32[24,1152]{1,0:T(8,128)S(1)}, u32[]{:S(2)}, u32[]{:S(2)}) %collective-permute-start.13) | collective-permute-done | bytes 110624 | tf_op jit(solution)/shard_map/ppermute | solution.py:37
  213.8 0.7 collective-permute-start.14
  214.5 5.1 %collective-permute-done.14 = f32[24,2304]{1,0:T(8,128)S(1)} collective-permute-done((f32[24,2304]{1,0:T(8,128)S(1)}, f32[24,2304]{1,0:T(8,128)S(1)}, u32[]{:S(2)}, u32[]{:S(2)}) %collective-permute-start.14) | collective-permute-done | bytes 221216 | tf_op jit(solution)/shard_map/ppermute | solution.py:37
  219.7 6.6 %collective-permute-start.15 = (f32[24,4608]{1,0:T(8,128)S(1)}, f32[24,4608]{1,0:T(8,128)S(1)}, u32[]{:S(2)}, u32[]{:S(2)}) collective-permute-start(f32[24,4608]{1,0:T(8,128)S(1)} %pad_maximum_fusion.2), channel_id=1, source_target_pairs={{0,8},{8,0},{1,9},{9,1},{2,10},{10,2},{3,11},{11,3},{4,12},{12,4},... | collective-permute-start | bytes 1327112 | tf_op jit(solution)/shard_map/ppermute | solution.py:37
  226.3 1.5 copy.19
  228.1 1.6 copy.20
  (63 shorter events, 2.1 us)
Async XLA Ops:
  5.1 0.7 copy-start.9
  6.1 4.7 %collective-permute-start = (f32[24,4608]{1,0:T(8,128)S(1)}, f32[24,4608]{1,0:T(8,128)S(1)}, u32[]{:S(2)}, u32[]{:S(2)}) collective-permute-start(f32[24,4608]{1,0:T(8,128)S(1)} %select_n.234), channel_id=1, source_target_pairs={{0,8},{8,0},{1,9},{9,1},{2,10},{10,2},{3,11},{11,3},{4,12},{12,4},... | collective-permute-start | bytes 1327112 | tf_op jit(solution)/shard_map/ppermute | solution.py:37
  11.0 6.7 %collective-permute-start.1 = (f32[24,2304]{1,0:T(8,128)S(1)}, f32[24,2304]{1,0:T(8,128)S(1)}, u32[]{:S(2)}, u32[]{:S(2)}) collective-permute-start(f32[24,2304]{1,0:T(8,128)S(1)} %slice_select_fusion.3), channel_id=1, source_target_pairs={{0,32},{32,0},{64,96},{96,64},{128,160},{160,128},{192,224},{224,1... | collective-permute-start | bytes 663560 | tf_op jit(solution)/shard_map/ppermute | solution.py:37
  17.8 3.7 %collective-permute-start.2 = (f32[24,1152]{1,0:T(8,128)S(1)}, f32[24,1152]{1,0:T(8,128)S(1)}, u32[]{:S(2)}, u32[]{:S(2)}) collective-permute-start(f32[24,1152]{1,0:T(8,128)S(1)} %slice_select_fusion.5), channel_id=1, source_target_pairs={{0,16},{16,0},{1,17},{17,1},{2,18},{18,2},{3,19},{19,3},{4,20},{20... | collective-permute-start | bytes 331784 | tf_op jit(solution)/shard_map/ppermute | solution.py:37
  21.5 5.8 %collective-permute-start.3 = (f32[24,1152]{1,0:T(8,128)S(1)}, f32[24,1152]{1,0:T(8,128)S(1)}, u32[]{:S(2)}, u32[]{:S(2)}) collective-permute-start(f32[24,1152]{1,0:T(8,128)S(1)} %select_add_fusion.3), channel_id=1, source_target_pairs={{0,64},{32,96},{64,0},{96,32},{128,192},{160,224},{192,128},{224,1... | collective-permute-start | bytes 331784 | tf_op jit(solution)/shard_map/ppermute | solution.py:37
  27.3 7.6 %collective-permute-start.4 = (f32[24,1152]{1,0:T(8,128)S(1)}, f32[24,1152]{1,0:T(8,128)S(1)}, u32[]{:S(2)}, u32[]{:S(2)}) collective-permute-start(f32[24,1152]{1,0:T(8,128)S(1)} %add.185), channel_id=1, source_target_pairs={{0,128},{32,160},{64,192},{96,224},{128,0},{160,32},{192,64},{224,... | collective-permute-start | bytes 331784 | tf_op jit(solution)/shard_map/ppermute | solution.py:37
  34.9 4.0 %collective-permute-start.5 = (f32[24,1152]{1,0:T(8,128)S(1)}, f32[24,1152]{1,0:T(8,128)S(1)}, u32[]{:S(2)}, u32[]{:S(2)}) collective-permute-start(f32[24,1152]{1,0:T(8,128)S(1)} %add.186), channel_id=1, source_target_pairs={{0,16},{16,0},{1,17},{17,1},{2,18},{18,2},{3,19},{19,3},{4,20},{20... | collective-permute-start | bytes 331784 | tf_op jit(solution)/shard_map/ppermute | solution.py:37
  38.9 11.8 %copy-start.8 = (f32[4,12,4608]{2,0,1:T(4,128)S(1)}, f32[4,12,4608]{2,0,1:T(4,128)}, u32[]{:S(2)}) copy-start(f32[4,12,4608]{2,0,1:T(4,128)} %param.10) | copy-start | bytes 2654212
  39.0 5.2 %collective-permute-start.6 = (f32[24,2304]{1,0:T(8,128)S(1)}, f32[24,2304]{1,0:T(8,128)S(1)}, u32[]{:S(2)}, u32[]{:S(2)}) collective-permute-start(f32[24,2304]{1,0:T(8,128)S(1)} %pad_maximum_fusion.3), channel_id=1, source_target_pairs={{0,32},{32,0},{64,96},{96,64},{128,160},{160,128},{192,224},{224,1... | collective-permute-start | bytes 663560 | tf_op jit(solution)/shard_map/ppermute | solution.py:37
  44.2 8.0 %collective-permute-start.7 = (f32[24,4608]{1,0:T(8,128)S(1)}, f32[24,4608]{1,0:T(8,128)S(1)}, u32[]{:S(2)}, u32[]{:S(2)}) collective-permute-start(f32[24,4608]{1,0:T(8,128)S(1)} %pad_maximum_fusion.1), channel_id=1, source_target_pairs={{0,8},{8,0},{1,9},{9,1},{2,10},{10,2},{3,11},{11,3},{4,12},{12,4},... | collective-permute-start | bytes 1327112 | tf_op jit(solution)/shard_map/ppermute | solution.py:37
  53.2 1.6 copy-start.3
  53.2 2.0 copy-start.4
  53.2 2.0 copy-start.6
  53.2 2.0 copy-start.7
  55.1 8.7 %copy-start = (f32[2,2,24,4608]{3,2,1,0:T(8,128)}, f32[2,2,24,4608]{3,2,1,0:T(8,128)S(1)}, u32[]{:S(2)}) copy-start(f32[2,2,24,4608]{3,2,1,0:T(8,128)S(1)} %maximum_maximum_fusion.chosen_ref) | copy-start | bytes 5308420
  63.8 48.4 %all-to-all-start = ((f32[8,96,1152]{2,1,0:T(8,128)}), f32[8,96,1152]{2,1,0:T(8,128)}, u32[]{:S(2)}, u32[]{:S(2)}) async-start(f32[8,96,1152]{2,1,0:T(8,128)} %shard_map.113), calls=%async_computation | async-start | bytes 7077888 | tf_op jit(solution)/shard_map/all_to_all | solution.py:366
  72.5 39.7 %copy-start.5 = (bf16[384,576]{1,0:T(8,128)(2,1)S(1)}, bf16[384,576]{1,0:T(8,128)(2,1)}, u32[]{:S(2)}) copy-start(bf16[384,576]{1,0:T(8,128)(2,1)} %constant.129.clone.table_ref) | copy-start | bytes 1327108
  124.2 48.1 %copy-start.1 = (bf16[768,768]{1,0:T(8,128)(2,1)S(1)}, bf16[768,768]{1,0:T(8,128)(2,1)}, u32[]{:S(2)}) copy-start(bf16[768,768]{1,0:T(8,128)(2,1)} %constant.130.clone.high_ref) | copy-start | bytes 3538948
  124.2 48.1 %copy-start.2 = (bf16[768,768]{1,0:T(8,128)(2,1)S(1)}, bf16[768,768]{1,0:T(8,128)(2,1)}, u32[]{:S(2)}) copy-start(bf16[768,768]{1,0:T(8,128)(2,1)} %constant.131.clone.low_ref) | copy-start | bytes 3538948
  182.2 3.5 %collective-permute-start.8 = (f32[24,4608]{1,0:T(8,128)S(1)}, f32[24,4608]{1,0:T(8,128)S(1)}, u32[]{:S(2)}, u32[]{:S(2)}) collective-permute-start(f32[24,4608]{1,0:T(8,128)S(1)} %select_bitcast_fusion), channel_id=1, source_target_pairs={{0,8},{8,0},{1,9},{9,1},{2,10},{10,2},{3,11},{11,3},{4,12},{12,4},... | collective-permute-start | bytes 1327112 | tf_op jit(solution)/shard_map/ppermute | solution.py:37
  185.8 6.7 %collective-permute-start.9 = (f32[24,2304]{1,0:T(8,128)S(1)}, f32[24,2304]{1,0:T(8,128)S(1)}, u32[]{:S(2)}, u32[]{:S(2)}) collective-permute-start(f32[24,2304]{1,0:T(8,128)S(1)} %slice_select_fusion.2), channel_id=1, source_target_pairs={{0,32},{32,0},{64,96},{96,64},{128,160},{160,128},{192,224},{224,1... | collective-permute-start | bytes 663560 | tf_op jit(solution)/shard_map/ppermute | solution.py:37
  192.6 3.7 %collective-permute-start.10 = (f32[24,1152]{1,0:T(8,128)S(1)}, f32[24,1152]{1,0:T(8,128)S(1)}, u32[]{:S(2)}, u32[]{:S(2)}) collective-permute-start(f32[24,1152]{1,0:T(8,128)S(1)} %slice_select_fusion.4), channel_id=1, source_target_pairs={{0,16},{16,0},{1,17},{17,1},{2,18},{18,2},{3,19},{19,3},{4,20},{20... | collective-permute-start | bytes 331784 | tf_op jit(solution)/shard_map/ppermute | solution.py:37
  196.3 5.8 %collective-permute-start.11 = (f32[24,1152]{1,0:T(8,128)S(1)}, f32[24,1152]{1,0:T(8,128)S(1)}, u32[]{:S(2)}, u32[]{:S(2)}) collective-permute-start(f32[24,1152]{1,0:T(8,128)S(1)} %select_add_fusion.2), channel_id=1, source_target_pairs={{0,64},{32,96},{64,0},{96,32},{128,192},{160,224},{192,128},{224,1... | collective-permute-start | bytes 331784 | tf_op jit(solution)/shard_map/ppermute | solution.py:37
  202.1 7.7 %collective-permute-start.12 = (f32[24,1152]{1,0:T(8,128)S(1)}, f32[24,1152]{1,0:T(8,128)S(1)}, u32[]{:S(2)}, u32[]{:S(2)}) collective-permute-start(f32[24,1152]{1,0:T(8,128)S(1)} %add.205), channel_id=1, source_target_pairs={{0,128},{32,160},{64,192},{96,224},{128,0},{160,32},{192,64},{224,... | collective-permute-start | bytes 331784 | tf_op jit(solution)/shard_map/ppermute | solution.py:37
  209.8 4.0 %collective-permute-start.13 = (f32[24,1152]{1,0:T(8,128)S(1)}, f32[24,1152]{1,0:T(8,128)S(1)}, u32[]{:S(2)}, u32[]{:S(2)}) collective-permute-start(f32[24,1152]{1,0:T(8,128)S(1)} %add.206), channel_id=1, source_target_pairs={{0,16},{16,0},{1,17},{17,1},{2,18},{18,2},{3,19},{19,3},{4,20},{20... | collective-permute-start | bytes 331784 | tf_op jit(solution)/shard_map/ppermute | solution.py:37
  213.8 5.8 %collective-permute-start.14 = (f32[24,2304]{1,0:T(8,128)S(1)}, f32[24,2304]{1,0:T(8,128)S(1)}, u32[]{:S(2)}, u32[]{:S(2)}) collective-permute-start(f32[24,2304]{1,0:T(8,128)S(1)} %pad_maximum_fusion.4), channel_id=1, source_target_pairs={{0,32},{32,0},{64,96},{96,64},{128,160},{160,128},{192,224},{224,1... | collective-permute-start | bytes 663560 | tf_op jit(solution)/shard_map/ppermute | solution.py:37
  219.7 8.1 %collective-permute-start.15 = (f32[24,4608]{1,0:T(8,128)S(1)}, f32[24,4608]{1,0:T(8,128)S(1)}, u32[]{:S(2)}, u32[]{:S(2)}) collective-permute-start(f32[24,4608]{1,0:T(8,128)S(1)} %pad_maximum_fusion.2), channel_id=1, source_target_pairs={{0,8},{8,0},{1,9},{9,1},{2,10},{10,2},{3,11},{11,3},{4,12},{12,4},... | collective-permute-start | bytes 1327112 | tf_op jit(solution)/shard_map/ppermute | solution.py:37
where the time goes:
time: 230 us
  waiting for transfers between devices  89.8 us (39%)
  blocking collectives  48.1 us (21%)
  starting transfers between devices  43.3 us (19%)
  Pallas kernels  30.5 us (13%)
  local copies, waits for them, and re-layouts  13.2 us (6%)
  other arithmetic  4.03 us (2%)
    ppermute x16, waiting for transfers between devices, swap(): return lax.ppermute(x, axis, [(i, i ^ bit) for i in range(size)])  52.3 us
    all_to_all x1, blocking collectives, per_device(): lax.all_to_all(columns, ('xh', 'y'), split_axis=0, concat_axis=0, tiled=T...  48.1 us
    all_to_all x1, waiting for transfers between devices, per_device(): lax.all_to_all(columns, ('xh', 'y'), split_axis=0, concat_axis=0, tiled=T...  37.5 us
    ppermute x16, starting transfers between devices, swap(): return lax.ppermute(x, axis, [(i, i ^ bit) for i in range(size)])  36.6 us
    pallas_call x1, Pallas kernels, screened(): pl.pallas_call(middle_kernel, out_shape=jax.ShapeDtypeStruct(values.shape...  11.9 us
    pallas_call x1, Pallas kernels, from_columns(): pl.pallas_call(inverse_kernel, out_shape=(jax.ShapeDtypeStruct((ROWS, POI...  9.86 us
    pallas_call x1, Pallas kernels, to_columns(): pl.pallas_call(forward_kernel, out_shape=jax.ShapeDtypeStruct((SLABS, ste...  8.66 us
    all_to_all x1, starting transfers between devices, per_device(): lax.all_to_all(columns, ('xh', 'y'), split_axis=0, concat_axis=0, tiled=T...  6.65 us
  transfers between devices with their start and end apart: 17, of which 16 were waited for; matrix products, arithmetic and copies ran while one was open for 3% of the time, Pallas kernels for 0%

commit v1 on v0

v1 whole, which is shorter than its diff:
```python
import functools
import math

import jax
import jax.numpy as jnp
import ml_dtypes
import numpy as np
from jax import lax
from jax.experimental import pallas as pl
from jax.experimental.pallas import tpu as pltpu
from jax.sharding import Mesh, PartitionSpec as P

NX = 48
NY = 96
NZ = 96
BLOC = 4
STEPS = 2
SLABS = 8
PLANES = NZ // SLABS
POINTS = NY * NX
ROWS = BLOC * PLANES
PAIR = 2 * PLANES
BLOCKS = 12
INNER = 8
LANES = INNER * NX
HALF = LANES // 2
COLUMNS = 3 * LANES
MIDDLE = POINTS // 2

length_first = 41.05
length_side = 41.05
length_last = 20.525
omega_screen = 0.106


def swap(x, axis, bit):
    size = lax.axis_size(axis)
    return lax.ppermute(x, axis, [(i, i ^ bit) for i in range(size)])


def near(x, bits):
    z_count, x_count = lax.axis_size("z"), lax.axis_size("xl")
    pairs = [
        (z * x_count + x, (z ^ (bits >> 1)) * x_count + (x ^ (bits & 1)))
        for z in range(z_count)
        for x in range(x_count)
    ]
    return lax.ppermute(x, ("z", "xl"), pairs)


def along(x, distance):
    size = lax.axis_size("z")
    return lax.ppermute(x, "z", [(i, (i + distance) % size) for i in range(size)])


def pick(pieces, index):
    low = jnp.where(index == 0, pieces[0], pieces[1])
    high = jnp.where(index == 2, pieces[2], pieces[3])
    return jnp.where(index < 2, low, high)


def tie(*values):
    return lax.optimization_barrier(values)


def join_cores(kept, sent):
    return kept + swap(sent, "c", 1)


def join_near(half):
    spot = lax.axis_index("z") % 2 * 2 + lax.axis_index("xl")
    width = half.shape[1] // 4
    quarters = [half[:, i * width : (i + 1) * width] for i in range(4)]
    arrived = [near(pick(quarters, spot ^ bits), bits) for bits in (1, 2, 3)]
    return pick(quarters, spot) + arrived[0] + arrived[1] + arrived[2]


def join_far(part):
    arrived = [along(part, distance) for distance in (2, 4, 6)]
    return part + arrived[0] + arrived[1] + arrived[2]


def spread_near(part):
    spot = lax.axis_index("z") % 2 * 2 + lax.axis_index("xl")
    quarters = [part] + [near(part, bits) for bits in (1, 2, 3)]
    return jnp.concatenate([pick(quarters, spot ^ i) for i in range(4)], axis=1)


def frequency(counter, length):
    return jnp.where(counter <= length // 2, counter, counter - length).astype(jnp.float32)


def coulomb_kernel(freq_z, freq_y, freq_x):
    squared = (
        (2.0 * math.pi / length_first * freq_z) ** 2
        + (2.0 * math.pi / length_side * freq_y) ** 2
        + (2.0 * math.pi / length_last * freq_x) ** 2
    )
    safe = jnp.where(squared > 0, squared, 1.0)
    screened = -4.0 * math.pi * jnp.expm1(-squared / (4.0 * omega_screen**2)) / safe
    return jnp.where(squared > 0, screened, math.pi / omega_screen**2)


def kernel_columns(xh, y):
    row = jnp.arange(2 * NZ)[:, None]
    lane = jnp.arange(COLUMNS)[None, :]
    kz = row // PAIR * PLANES + row % PLANES
    kb = 3 * y + lane // LANES
    kk = 4 * xh + lane % HALF // NX
    return coulomb_kernel(
        frequency(kz, NZ), frequency(kb + BLOCKS * kk, NY), frequency(lane % NX, NX)
    ) * (1.0 / (NX * NY * NZ))


def split_table(table):
    high = table.astype(ml_dtypes.bfloat16)
    low = (table - high.astype(np.float64)).astype(ml_dtypes.bfloat16)
    return high, low


@functools.cache
def tables():
    inner, x = np.divmod(np.arange(LANES), NX)
    angle = -2.0 * np.pi * (
        (inner[:, None] * inner[None, :] % INNER) / INNER + (x[:, None] * x[None, :] % NX) / NX
    )
    real, imag = np.cos(angle), np.sin(angle)
    forward = np.zeros((2, LANES, 2, 2, HALF))
    inverse = np.zeros((2, 2, HALF, 2, LANES))
    for half in range(2):
        part = slice(half * HALF, (half + 1) * HALF)
        forward[0, :, half, 0], forward[1, :, half, 0] = real[:, part], -imag[:, part]
        forward[0, :, half, 1], forward[1, :, half, 1] = imag[:, part], real[:, part]
        inverse[half, 0, :, 0], inverse[half, 1, :, 0] = real[part], imag[part]
        inverse[half, 0, :, 1], inverse[half, 1, :, 1] = -imag[part], real[part]
    forward = split_table(forward.reshape(2 * LANES, 2 * LANES))
    inverse = split_table(inverse.reshape(2 * LANES, 2 * LANES))
    turn = -2.0 * np.pi / NY * (np.arange(BLOCKS)[:, None] * inner[None, :] % NY)
    twiddle = np.cos(turn).astype(np.float32), np.sin(turn).astype(np.float32)
    slab, rest = np.divmod(np.arange(2 * NZ), PAIR)
    band, plane = np.divmod(rest, PLANES)
    z = slab * PLANES + plane
    same = band[:, None] == band[None, :]
    angle = 2.0 * np.pi / NZ * (z[:, None] * z[None, :] % NZ)
    stacked = np.concatenate([np.where(same, np.cos(angle), 0), np.where(same, np.sin(angle), 0)])
    high, low = split_table(stacked)
    along_z = np.concatenate([high, high, low], axis=1)
    return forward, inverse, twiddle, along_z


def split(x):
    high = x.astype(jnp.bfloat16)
    return high, (x - high.astype(jnp.float32)).astype(jnp.bfloat16)


def dot(a, b):
    return lax.dot_general(a, b, (((1,), (0,)), ((), ())), preferred_element_type=jnp.float32)


def dft12(values, sign):
    def turn(value):
        re, im = value
        return (-im, re) if sign > 0 else (im, -re)

    def add(a, b):
        return a[0] + b[0], a[1] + b[1]

    def sub(a, b):
        return a[0] - b[0], a[1] - b[1]

    quarter = []
    for n1 in range(3):
        a = [values[(4 * n1 + 3 * n2) % 12] for n2 in range(4)]
        even, odd = add(a[0], a[2]), add(a[1], a[3])
        left, right = sub(a[0], a[2]), turn(sub(a[1], a[3]))
        quarter.append([add(even, odd), add(left, right), sub(even, odd), sub(left, right)])
    result = [None] * 12
    for k4 in range(4):
        b = [quarter[n1][k4] for n1 in range(3)]
        total = add(b[1], b[2])
        difference = sub(b[1], b[2])
        middle = (b[0][0] - 0.5 * total[0], b[0][1] - 0.5 * total[1])
        scale = math.sqrt(0.75)
        side = turn((scale * difference[0], scale * difference[1]))
        for k3, value in enumerate((add(b[0], total), add(middle, side), sub(middle, side))):
            where = next(k for k in range(12) if k % 3 == k3 and k % 4 == k4)
            result[where] = value
    return result


def forward_kernel(
    here_ref, orbital_ref, half_ref, other_ref, cos_ref, sin_ref, high_source, low_source,
    out_ref, chosen_ref, field, field_high, field_low, high_ref, low_ref, loaded,
):
    loads = [
        pltpu.make_async_copy(source, target, loaded.at[index])
        for index, (source, target) in enumerate(((high_source, high_ref), (low_source, low_ref)))
    ]
    for load in loads:
        load.start()
    core = here_ref[1]
    for step in range(STEPS):
        for offset in range(0, MIDDLE, LANES):
            for where, source in ((core, half_ref), (1 - core, other_ref)):
                lanes = pl.ds(pl.multiple_of(where * MIDDLE + offset, 128), LANES)
                for a in range(2):
                    first = (step * 2 + a) * PLANES
                    rows = source[first : first + PLANES, offset : offset + LANES]
                    chosen_ref[step, a, :, lanes] = jnp.concatenate([rows, rows], axis=0)

    for step in range(STEPS):

        def tile(index, carry):
            for group in range(2):
                for part in range(3):
                    rows = pl.ds(pl.multiple_of(group * PAIR + index * 8, 8), 8)
                    own = pl.ds(pl.multiple_of(index * 8, 8), 8)
                    values = []
                    for block in range(BLOCKS):
                        lanes = pl.ds(block * LANES + part * 128, 128)
                        orbital = orbital_ref[rows, lanes]
                        values.append(
                            (orbital * chosen_ref[step, 0, own, lanes], orbital * chosen_ref[step, 1, own, lanes])
                        )
                    values = dft12(values, -1)
                    for kb, (re, im) in enumerate(values):
                        cosine = cos_ref[kb : kb + 1, part * 128 : part * 128 + 128]
                        sine = sin_ref[kb : kb + 1, part * 128 : part * 128 + 128]
                        to = pl.ds(pl.multiple_of(kb * ROWS + group * PAIR + index * 8, 8), 8)
                        field[to, pl.ds(part * 128, 128)] = re * cosine - im * sine
                        field[to, pl.ds(LANES + part * 128, 128)] = re * sine + im * cosine
            return carry

        lax.fori_loop(0, PAIR // 8, tile, 0)
        field_high[...], field_low[...] = split(field[...])
        if step == 0:
            for load in loads:
                load.wait()
        for piece in range(3):
            lanes = pl.ds(piece * 256, 256)
            high = high_ref[:, lanes]
            result = dot(field_high[...], high) + dot(field_low[...], high) + dot(field_high[...], low_ref[:, lanes])
            for part in range(2):
                half, offset = divmod(2 * piece + part, 3)
                for kb in range(BLOCKS):
                    column, turn = divmod(kb, 3)
                    out_ref[
                        half * 4 + column, pl.ds(step * ROWS, ROWS), pl.ds(turn * LANES + offset * 128, 128)
                    ] = result[kb * ROWS : kb * ROWS + ROWS, part * 128 : part * 128 + 128]


def middle_kernel(step, value_ref, kernel_ref, table_ref, out_ref):
    imaginary = lax.broadcasted_iota(jnp.int32, (2 * NZ, LANES), 1) >= HALF

    def swapped(x):
        return jnp.concatenate([x[:, HALF:], x[:, :HALF]], axis=1)

    def transform(x, sign):
        high, low = split(x)
        both = dot(table_ref[...], jnp.concatenate([high, low, high], axis=0))
        cosine, sine = both[: 2 * NZ], swapped(both[2 * NZ :])
        return cosine + jnp.where(imaginary, -sign * sine, sign * sine)

    for group in range(ROWS // PAIR):
        source = slice(step * ROWS + group * PAIR, step * ROWS + group * PAIR + PAIR)
        own = slice(group * PAIR, group * PAIR + PAIR)
        for turn in range(3):
            lanes = slice(turn * LANES, turn * LANES + LANES)
            x = jnp.concatenate([value_ref[slab, source, lanes] for slab in range(SLABS)], axis=0)
            x = transform(x, 1.0) * kernel_ref[:, lanes]
            x = transform(x, -1.0)
            for slab in range(SLABS):
                out_ref[slab, own, lanes] = x[slab * PAIR : slab * PAIR + PAIR]


def inverse_kernel(
    step, here_ref, value_ref, orbital_ref, chosen_ref, cos_ref, sin_ref, high_source, low_source, *rest
):
    if step == 0:
        applied_ref, kept_ref, sent_ref, field_high, field_low, field, totals, high_ref, low_ref, loaded = rest
        sums = applied_ref
    else:
        before_ref, applied_ref, kept_ref, sent_ref, field_high, field_low, field, totals, high_ref, low_ref, loaded, sums = rest
    loads = [
        pltpu.make_async_copy(source, target, loaded.at[index])
        for index, (source, target) in enumerate(((high_source, high_ref), (low_source, low_ref)))
    ]
    for load in loads:
        load.start()
    for kb in range(BLOCKS):
        column, turn = divmod(kb, 3)
        for half in range(2):
            x = value_ref[half * 4 + column, :, pl.ds(turn * LANES, LANES)]
            high, low = split(x)
            field_high[kb * ROWS : kb * ROWS + ROWS, half * LANES : half * LANES + LANES] = high
            field_low[kb * ROWS : kb * ROWS + ROWS, half * LANES : half * LANES + LANES] = low
    for load in loads:
        load.wait()
    for piece in range(3):
        lanes = pl.ds(piece * 256, 256)
        high = high_ref[:, lanes]
        field[:, lanes] = (
            dot(field_high[...], high) + dot(field_low[...], high) + dot(field_high[...], low_ref[:, lanes])
        )

    def tile(index, carry):
        own = pl.ds(pl.multiple_of(index * 8, 8), 8)
        for part in range(3):
            for group in range(2):
                rows = pl.ds(pl.multiple_of(group * PAIR + index * 8, 8), 8)
                values = []
                for kb in range(BLOCKS):
                    cosine = cos_ref[kb : kb + 1, part * 128 : part * 128 + 128]
                    sine = sin_ref[kb : kb + 1, part * 128 : part * 128 + 128]
                    at = pl.ds(pl.multiple_of(kb * ROWS + group * PAIR + index * 8, 8), 8)
                    re = field[at, pl.ds(part * 128, 128)]
                    im = field[at, pl.ds(LANES + part * 128, 128)]
                    values.append((re * cosine + im * sine, im * cosine - re * sine))
                values = dft12(values, 1)
                for block, (first, second) in enumerate(values):
                    lanes = pl.ds(block * LANES + part * 128, 128)
                    orbital = orbital_ref[rows, lanes]
                    applied = first * chosen_ref[step, 0, own, lanes] + second * chosen_ref[step, 1, own, lanes]
                    if step == 0:
                        sums[rows, lanes] = applied
                    else:
                        sums[rows, lanes] = before_ref[rows, lanes] + applied
                    if group == 0:
                        totals[0, own, lanes] = first * orbital
                        totals[1, own, lanes] = second * orbital
                    else:
                        totals[0, own, lanes] += first * orbital
                        totals[1, own, lanes] += second * orbital
        return carry

    lax.fori_loop(0, PAIR // 8, tile, 0)
    core = here_ref[1]
    for offset in range(0, MIDDLE, LANES):
        for where, target in ((core, kept_ref), (1 - core, sent_ref)):
            lanes = pl.ds(pl.multiple_of(where * MIDDLE + offset, 128), LANES)
            first = totals[0, :PLANES, lanes] + totals[0, PLANES:, lanes]
            second = totals[1, :PLANES, lanes] + totals[1, PLANES:, lanes]
            target[:, offset : offset + LANES] = jnp.concatenate([first, second], axis=0)
    if step:
        for block in range(BLOCKS):
            lanes = pl.ds(block * LANES, LANES)
            for band in range(BLOC):
                applied_ref[:, band, lanes] = sums[band * PLANES : band * PLANES + PLANES, lanes]


def pick_kernel(here_ref, owner_ref, picks_ref, orbital_ref, flat_ref, kept_ref, sent_ref):
    core = here_ref[1]
    for offset in range(0, POINTS, LANES):
        lanes = pl.ds(offset, LANES)
        for band in range(BLOC):
            flat_ref[band * PLANES : band * PLANES + PLANES, lanes] = orbital_ref[:, band, lanes]
    for step in range(STEPS):
        mine = owner_ref[step] == here_ref[0]
        for offset in range(0, MIDDLE, LANES):
            for where, target in ((core, kept_ref), (1 - core, sent_ref)):
                lanes = pl.ds(pl.multiple_of(where * MIDDLE + offset, 128), LANES)
                bands = [flat_ref[band * PLANES : band * PLANES + PLANES, lanes] for band in range(BLOC)]
                pair = [pick(bands, picks_ref[step, a]) for a in range(2)]
                target[step * PAIR : step * PAIR + PAIR, offset : offset + LANES] = jnp.where(mine, jnp.concatenate(pair, axis=0), 0.0)


def place_kernel(here_ref, own_ref, other_ref, out_ref):
    core = here_ref[1]
    for step in range(STEPS):
        for offset in range(0, MIDDLE, LANES):
            for where, source in ((core, own_ref), (1 - core, other_ref)):
                lanes = pl.ds(pl.multiple_of(where * MIDDLE + offset, 128), LANES)
                for a in range(2):
                    first = (step * 2 + a) * PLANES
                    out_ref[step, :, a, lanes] = source[first : first + PLANES, offset : offset + LANES]


PARAMS = dict(compiler_params=pltpu.CompilerParams(vmem_limit_bytes=48 * 1024 * 1024))
VMEM = pl.BlockSpec(memory_space=pltpu.VMEM)
SMEM = pl.BlockSpec(memory_space=pltpu.SMEM)
HBM = pl.BlockSpec(memory_space=pltpu.HBM)


def cost(operations, size):
    return pl.CostEstimate(flops=operations, bytes_accessed=size, transcendentals=0)


BOTH_SHAPE = jax.ShapeDtypeStruct((STEPS * PAIR, MIDDLE), jnp.float32)
HALF_SHAPE = jax.ShapeDtypeStruct((PAIR, MIDDLE), jnp.float32)


def pick_orbitals(here, owner, picks, orbitals):
    return pl.pallas_call(
        pick_kernel,
        out_shape=(jax.ShapeDtypeStruct((ROWS, POINTS), jnp.float32),) + (BOTH_SHAPE,) * 2,
        in_specs=[SMEM] * 3 + [VMEM],
        out_specs=(VMEM,) * 3,
        cost_estimate=cost(0, 4_000_000),
        **PARAMS,
    )(here, owner, picks, orbitals)


def place(here, own, other):
    return pl.pallas_call(
        place_kernel,
        out_shape=jax.ShapeDtypeStruct((STEPS, PLANES, 2, POINTS), jnp.float32),
        in_specs=[SMEM] + [VMEM] * 2,
        out_specs=VMEM,
        cost_estimate=cost(0, 2_000_000),
        **PARAMS,
    )(here, own, other)


TABLE_SCRATCH = [
    pltpu.VMEM((2 * LANES, 2 * LANES), jnp.bfloat16),
    pltpu.VMEM((2 * LANES, 2 * LANES), jnp.bfloat16),
    pltpu.SemaphoreType.DMA((2,)),
]


def to_columns(here, orbitals, half, other):
    forward, _, twiddle, _ = tables()
    tall = BLOCKS * ROWS
    return pl.pallas_call(
        forward_kernel,
        out_shape=(
            jax.ShapeDtypeStruct((SLABS, STEPS * ROWS, COLUMNS), jnp.float32),
            jax.ShapeDtypeStruct((STEPS, 2, PAIR, POINTS), jnp.float32),
        ),
        in_specs=[SMEM] + [VMEM] * 5 + [HBM] * 2,
        out_specs=(VMEM, VMEM),
        scratch_shapes=[
            pltpu.VMEM((tall, 2 * LANES), jnp.float32),
            pltpu.VMEM((tall, 2 * LANES), jnp.bfloat16),
            pltpu.VMEM((tall, 2 * LANES), jnp.bfloat16),
        ]
        + TABLE_SCRATCH,
        cost_estimate=cost(12 * tall * (2 * LANES) ** 2, 4_000_000),
        **PARAMS,
    )(here, orbitals, half, other, *twiddle, *forward)


def screened(values, kernel, step):
    _, _, _, along_z = tables()
    return pl.pallas_call(
        functools.partial(middle_kernel, step),
        out_shape=jax.ShapeDtypeStruct((SLABS, ROWS, COLUMNS), jnp.float32),
        in_specs=[VMEM] * 3,
        out_specs=VMEM,
        cost_estimate=cost(2 * 4 * 4 * NZ * 6 * NZ * COLUMNS, 4_000_000),
        **PARAMS,
    )(values, kernel, along_z)


def from_columns(here, values, orbitals, chosen, step, before=None):
    _, inverse, twiddle, _ = tables()
    tall = BLOCKS * ROWS
    first_step = before is None
    applied = (ROWS, POINTS) if first_step else (PLANES, BLOC, POINTS)
    return pl.pallas_call(
        functools.partial(inverse_kernel, step),
        out_shape=(jax.ShapeDtypeStruct(applied, jnp.float32), HALF_SHAPE, HALF_SHAPE),
        in_specs=[SMEM] + [VMEM] * 5 + [HBM] * 2 + ([] if first_step else [VMEM]),
        out_specs=(VMEM,) * 3,
        scratch_shapes=[
            pltpu.VMEM((tall, 2 * LANES), jnp.bfloat16),
            pltpu.VMEM((tall, 2 * LANES), jnp.bfloat16),
            pltpu.VMEM((tall, 2 * LANES), jnp.float32),
            pltpu.VMEM((2, PAIR, POINTS), jnp.float32),
        ]
        + TABLE_SCRATCH
        + ([] if first_step else [pltpu.VMEM((ROWS, POINTS), jnp.float32)]),
        cost_estimate=cost(6 * tall * (2 * LANES) ** 2, 8_000_000),
        **PARAMS,
    )(here, values, orbitals, chosen, *twiddle, *inverse, *(() if first_step else (before,)))


def exchange(columns):
    return lax.all_to_all(columns, ("xh", "y"), split_axis=0, concat_axis=0, tiled=True)


def per_device(orbitals, owner, picks):
    core = lax.axis_index("c")
    group = (lax.axis_index("z") * 2 + lax.axis_index("xl")) * 2 + core
    here = jnp.stack([group, core]).astype(jnp.int32)
    flat, kept, sent = pick_orbitals(here, owner, picks, orbitals.transpose(1, 0, 2))
    half = spread_near(join_far(join_near(join_cores(kept, sent))))
    other = swap(half, "c", 1)
    columns, chosen = to_columns(here, flat, half, other)
    columns, xh, y = tie(columns, lax.axis_index("xh"), lax.axis_index("y"))
    kernel = kernel_columns(xh, y)
    forward = exchange(columns)
    backward = [exchange(screened(forward, kernel, step)) for step in range(STEPS)]
    applied, kept, sent = from_columns(here, backward[0], flat, chosen, 0)
    part = join_near(join_cores(kept, sent))
    last, part = tie(backward[1], part)
    applied, kept, sent = from_columns(here, last, flat, chosen, 1, applied)
    part = jnp.concatenate([part, join_near(join_cores(kept, sent))], axis=0)
    half = spread_near(join_far(part))
    other = swap(half, "c", 1)
    return applied.transpose(1, 0, 2), place(here, half, other).transpose(0, 2, 1, 3)


def solution(mesh):
    fine = Mesh(mesh.devices.reshape(8, 2, 2, 2, 4), ("z", "xl", "c", "xh", "y"))
    band, slab = ("z", "xl", "c"), ("xh", "y")
    in_specs = (P(band, slab, None), P(), P())
    out_specs = (P(band, slab, None), P(None, None, slab, None))
    return jax.shard_map(
        per_device, mesh=fine, in_specs=in_specs, out_specs=out_specs, check_vma=False
    )
```

time: 230 us -> 221 us (0.961)
  blocking collectives: 48.1 us -> 0 us
  waiting for transfers between devices: 89.8 us -> 112 us
  starting transfers between devices: 43.3 us -> 56.5 us
  Pallas kernels: 30.5 us -> 42.2 us
  local copies, waits for them, and re-layouts: 13.2 us -> 7.46 us
    ppermute x0 -> x21, waiting for transfers between devices: none -> 48.5 us  [the longest x15 30.1 us: near(): return lax.ppermute(x, ('z', 'xl'), pairs)]
    all_to_all x1 -> x0, blocking collectives: 48.1 us -> none  [per_device(): lax.all_to_all(columns, ('xh', 'y'), split_axis=0, concat_axis=0, tiled=T...]
    ppermute x16 -> x5, waiting for transfers between devices: 52.3 us -> 6.47 us  [swap(): return lax.ppermute(x, axis, [(i, i ^ bit) for i in range(size)])]
    ppermute x0 -> x21, starting transfers between devices: none -> 29.9 us  [the longest x15 15.7 us: near(): return lax.ppermute(x, ('z', 'xl'), pairs)]
    ppermute x16 -> x5, starting transfers between devices: 36.6 us -> 9.58 us  [swap(): return lax.ppermute(x, axis, [(i, i ^ bit) for i in range(size)])]
    all_to_all x1 -> x3, waiting for transfers between devices: 37.5 us -> 56.5 us  [exchange(): lax.all_to_all(columns, ('xh', 'y'), split_axis=0, concat_axis=0, tiled=T...]
    pallas_call x3 -> x7, Pallas kernels: 30.5 us -> 42.2 us  [the longest x2 16.9 us: screened(): pl.pallas_call(functools.partial(middle_kernel, step), out_shape=jax.Shap...]
    all_to_all x1 -> x3, starting transfers between devices: 6.65 us -> 17.1 us  [exchange(): lax.all_to_all(columns, ('xh', 'y'), split_axis=0, concat_axis=0, tiled=T...]
  transfers between devices with their start and end apart: 17 -> 29, of which waited for: 16 -> 24; matrix products, arithmetic and copies ran while one was open for 3% -> 0% of each run, Pallas kernels for 0% -> 6%
where the time goes in v1:
time: 221 us
  waiting for transfers between devices  112 us (51%)
  starting transfers between devices  56.5 us (26%)
  Pallas kernels  42.2 us (19%)
  local copies, waits for them, and re-layouts  7.46 us (3%)
    all_to_all x3, waiting for transfers between devices, exchange(): lax.all_to_all(columns, ('xh', 'y'), split_axis=0, concat_axis=0, tiled=T...  56.5 us
    ppermute x15, waiting for transfers between devices, near(): return lax.ppermute(x, ('z', 'xl'), pairs)  30.1 us
    ppermute x6, waiting for transfers between devices, along(): lax.ppermute(x, 'z', [(i, (i + distance) % size) for i in range(size)])  18.4 us
    all_to_all x3, starting transfers between devices, exchange(): lax.all_to_all(columns, ('xh', 'y'), split_axis=0, concat_axis=0, tiled=T...  17.1 us
    pallas_call x2, Pallas kernels, screened(): pl.pallas_call(functools.partial(middle_kernel, step), out_shape=jax.Shap...  16.9 us
    ppermute x15, starting transfers between devices, near(): return lax.ppermute(x, ('z', 'xl'), pairs)  15.7 us
    ppermute x6, starting transfers between devices, along(): lax.ppermute(x, 'z', [(i, (i + distance) % size) for i in range(size)])  14.2 us
    pallas_call x2, Pallas kernels, from_columns(): pl.pallas_call(functools.partial(inverse_kernel, step), out_shape=(jax.Sh...  12.6 us
  transfers between devices with their start and end apart: 29, of which 24 were waited for; matrix products, arithmetic and copies ran while one was open for 0% of the time, Pallas kernels for 6%

profile of v1, /device:TPU:1, one launch (start us, length us, event | category | flops | bytes accessed | tf_op | source)
XLA Modules:
  0.0 220.5 jit_solution(17276279553766519290)
XLA Ops:
  0.7 1.2 copy-done.3
  4.3 3.3 %collective-permute-start = (f32[48,2304]{1,0:T(8,128)S(1)}, f32[48,2304]{1,0:T(8,128)S(1)}, u32[]{:S(2)}, u32[]{:S(2)}) collective-permute-start(f32[48,2304]{1,0:T(8,128)S(1)} %get-tuple-element.20), channel_id=1, source_target_pairs={{0,8},{8,0},{1,9},{9,1},{2,10},{10,2},{3,11},{11,3},{4,12},{12,4},... | collective-permute-start | bytes 1327112 | tf_op jit(solution)/shard_map/ppermute | solution.py:38
  7.6 1.4 collective-permute-done
  10.6 1.6 collective-permute-start.2
  12.2 2.6 %collective-permute-done.3 = f32[48,576]{1,0:T(8,128)S(1)} collective-permute-done((f32[48,576]{1,0:T(8,128)S(1)}, f32[48,576]{1,0:T(8,128)S(1)}, u32[]{:S(2)}, u32[]{:S(2)}) %collective-permute-start.3) | collective-permute-done | bytes 110624 | tf_op jit(solution)/shard_map/ppermute | solution.py:48
  14.7 3.3 %collective-permute-done.1 = f32[48,576]{1,0:T(8,128)S(1)} collective-permute-done((f32[48,576]{1,0:T(8,128)S(1)}, f32[48,576]{1,0:T(8,128)S(1)}, u32[]{:S(2)}, u32[]{:S(2)}) %collective-permute-start.1) | collective-permute-done | bytes 110624 | tf_op jit(solution)/shard_map/ppermute | solution.py:48
  18.2 4.4 %collective-permute-start.6 = (f32[48,576]{1,0:T(8,128)S(1)}, f32[48,576]{1,0:T(8,128)S(1)}, u32[]{:S(2)}, u32[]{:S(2)}) collective-permute-start(f32[48,576]{1,0:T(8,128)S(1)} %add_add_fusion.2), channel_id=1, source_target_pairs={{0,192},{32,224},{64,0},{96,32},{128,64},{160,96},{192,128},{224,1... | collective-permute-start | bytes 331784 | tf_op jit(solution)/shard_map/ppermute | solution.py:53
  23.6 2.3 %collective-permute-start.4 = (f32[48,576]{1,0:T(8,128)S(1)}, f32[48,576]{1,0:T(8,128)S(1)}, u32[]{:S(2)}, u32[]{:S(2)}) collective-permute-start(f32[48,576]{1,0:T(8,128)S(1)} %add_add_fusion.2), channel_id=1, source_target_pairs={{0,64},{32,96},{64,128},{96,160},{128,192},{160,224},{192,0},{224,... | collective-permute-start | bytes 331784 | tf_op jit(solution)/shard_map/ppermute | solution.py:53
  26.8 6.8 %collective-permute-done.5 = f32[48,576]{1,0:T(8,128)S(1)} collective-permute-done((f32[48,576]{1,0:T(8,128)S(1)}, f32[48,576]{1,0:T(8,128)S(1)}, u32[]{:S(2)}, u32[]{:S(2)}) %collective-permute-start.5) | collective-permute-done | bytes 110624 | tf_op jit(solution)/shard_map/ppermute | solution.py:53
  33.7 4.0 %collective-permute-start.9 = (f32[48,576]{1,0:T(8,128)S(1)}, f32[48,576]{1,0:T(8,128)S(1)}, u32[]{:S(2)}, u32[]{:S(2)}) collective-permute-start(f32[48,576]{1,0:T(8,128)S(1)} %add_add_fusion.1), channel_id=1, source_target_pairs={{0,48},{16,32},{32,16},{48,0},{64,112},{80,96},{96,80},{112,64},{1... | collective-permute-start | bytes 331784 | tf_op jit(solution)/shard_map/ppermute | solution.py:48
  38.0 1.9 collective-permute-done.9
  39.9 2.7 %collective-permute-done.8 = f32[48,576]{1,0:T(8,128)S(1)} collective-permute-done((f32[48,576]{1,0:T(8,128)S(1)}, f32[48,576]{1,0:T(8,128)S(1)}, u32[]{:S(2)}, u32[]{:S(2)}) %collective-permute-start.8) | collective-permute-done | bytes 110624 | tf_op jit(solution)/shard_map/ppermute | solution.py:48
  43.2 1.8 collective-permute-start.10
  45.0 1.4 collective-permute-done.10.other_ref
  46.4 1.3 copy-done.11
  47.7 10.0 %shard_map.114 = (f32[8,96,1152]{2,1,0:T(8,128)}, f32[2,2,24,4608]{3,2,1,0:T(8,128)S(1)}) custom-call(s32[2]{0:T(128)S(1)} %pad_add_fusion.here_ref, f32[48,4608]{1,0:T(8,128)S(1)} %get-tuple-element.18.orbital_ref, f32[48,2304]{1,0:T(8,128)S(1)} %concatenate.9.half_ref, f32[48,2304]{1,0:T(8,128)S(1)} %collective-permute-done.10.other_ref, ...), custom_call_target="tpu_custom_call" | custom-call | flops 4076863488 | bytes 4000000 | tf_op jit(solution)/shard_map/pallas_call | solution.py:424
  57.7 1.3 copy-done
  59.0 6.7 %all-to-all-start = ((f32[8,96,1152]{2,1,0:T(8,128)}), f32[8,96,1152]{2,1,0:T(8,128)}, u32[]{:S(2)}, u32[]{:S(2)}) async-start(f32[8,96,1152]{2,1,0:T(8,128)} %get-tuple-element.22), calls=%async_computation | async-start | bytes 7077888 | tf_op jit(solution)/shard_map/all_to_all | solution.py:479
  66.4 41.1 %all-to-all-done.value_ref = f32[8,96,1152]{2,1,0:T(8,128)} async-done(((f32[8,96,1152]{2,1,0:T(8,128)}), f32[8,96,1152]{2,1,0:T(8,128)}, u32[]{:S(2)}, u32[]{:S(2)}) %all-to-all-start) | async-done | bytes 3538976 | tf_op jit(solution)/shard_map/all_to_all | solution.py:479
  107.5 8.4 %shard_map.116 = f32[8,48,1152]{2,1,0:T(8,128)} custom-call(f32[8,96,1152]{2,1,0:T(8,128)} %all-to-all-done.value_ref, f32[192,1152]{1,0:T(8,128)S(1)} %fusion.1.kernel_ref, bf16[384,576]{1,0:T(8,128)(2,1)S(1)} %copy-done.12), custom_call_target="tpu_custom_call" | custom-call | flops 2038431744 | bytes 4000000 | tf_op jit(solution)/shard_map/pallas_call | solution.py:445
  115.9 5.2 %all-to-all-start.2 = ((f32[8,48,1152]{2,1,0:T(8,128)}), f32[8,48,1152]{2,1,0:T(8,128)}, u32[]{:S(2)}, u32[]{:S(2)}) async-start(f32[8,48,1152]{2,1,0:T(8,128)} %shard_map.116), calls=%async_computation.2 | async-start | bytes 3538944 | tf_op jit(solution)/shard_map/all_to_all | solution.py:479
  121.1 8.4 %shard_map.115 = f32[8,48,1152]{2,1,0:T(8,128)} custom-call(f32[8,96,1152]{2,1,0:T(8,128)} %all-to-all-done.value_ref, f32[192,1152]{1,0:T(8,128)S(1)} %fusion.1.kernel_ref, bf16[384,576]{1,0:T(8,128)(2,1)S(1)} %copy-done.12), custom_call_target="tpu_custom_call" | custom-call | flops 2038431744 | bytes 4000000 | tf_op jit(solution)/shard_map/pallas_call | solution.py:445
  129.5 14.3 %all-to-all-done.2.value_ref = f32[8,48,1152]{2,1,0:T(8,128)} async-done(((f32[8,48,1152]{2,1,0:T(8,128)}), f32[8,48,1152]{2,1,0:T(8,128)}, u32[]{:S(2)}, u32[]{:S(2)}) %all-to-all-start.2) | async-done | bytes 1769504 | tf_op jit(solution)/shard_map/all_to_all | solution.py:479
  143.9 5.2 %all-to-all-start.1 = ((f32[8,48,1152]{2,1,0:T(8,128)}), f32[8,48,1152]{2,1,0:T(8,128)}, u32[]{:S(2)}, u32[]{:S(2)}) async-start(f32[8,48,1152]{2,1,0:T(8,128)} %shard_map.115), calls=%async_computation.1 | async-start | bytes 3538944 | tf_op jit(solution)/shard_map/all_to_all | solution.py:479
  149.1 5.8 %shard_map.117 = (f32[48,4608]{1,0:T(8,128)S(1)}, f32[24,2304]{1,0:T(8,128)S(1)}, f32[24,2304]{1,0:T(8,128)S(1)}) custom-call(s32[2]{0:T(128)S(1)} %pad_add_fusion.here_ref, f32[8,48,1152]{2,1,0:T(8,128)} %all-to-all-done.2.value_ref, f32[48,4608]{1,0:T(8,128)S(1)} %get-tuple-element.18.orbital_ref, f32[2,2,24,4608]{3,2,1,0:T(8,128)} %copy-done, ...), custom_call_target="tpu_custom_call" | custom-call | flops 2038431744 | bytes 8000000 | tf_op jit(solution)/shard_map/pallas_call | solution.py:460
  156.5 1.1 collective-permute-done.11
  157.7 1.7 collective-permute-start.14
  159.5 1.3 collective-permute-start.12
  160.9 1.5 collective-permute-done.14
  162.4 9.0 %collective-permute-done.12 = f32[24,576]{1,0:T(8,128)S(1)} collective-permute-done((f32[24,576]{1,0:T(8,128)S(1)}, f32[24,576]{1,0:T(8,128)S(1)}, u32[]{:S(2)}, u32[]{:S(2)}) %collective-permute-start.12) | collective-permute-done | bytes 55328 | tf_op jit(solution)/shard_map/ppermute | solution.py:48
  172.6 1.2 copy-done.5
  173.8 6.8 %shard_map.118 = (f32[12,4,4608]{2,1,0:T(4,128)}, f32[24,2304]{1,0:T(8,128)S(1)}, f32[24,2304]{1,0:T(8,128)S(1)}) custom-call(s32[2]{0:T(128)S(1)} %pad_add_fusion.here_ref, f32[8,48,1152]{2,1,0:T(8,128)} %all-to-all-done.1.value_ref, f32[48,4608]{1,0:T(8,128)S(1)} %get-tuple-element.18.orbital_ref, f32[2,2,24,4608]{3,2,1,0:T(8,128)} %copy-done, ...), custom_call_target="tpu_custom_call" | custom-call | flops 2038431744 | bytes 8000000 | tf_op jit(solution)/shard_map/pallas_call | solution.py:460
  180.6 2.4 %collective-permute-start.15 = (f32[24,2304]{1,0:T(8,128)S(1)}, f32[24,2304]{1,0:T(8,128)S(1)}, u32[]{:S(2)}, u32[]{:S(2)}) collective-permute-start(f32[24,2304]{1,0:T(8,128)S(1)} %get-tuple-element.33), channel_id=1, source_target_pairs={{0,8},{8,0},{1,9},{9,1},{2,10},{10,2},{3,11},{11,3},{4,12},{12,4},... | collective-permute-start | bytes 663560 | tf_op jit(solution)/shard_map/ppermute | solution.py:38
  183.0 1.1 collective-permute-done.15
  184.4 1.5 collective-permute-start.18
  185.8 1.2 collective-permute-start.16
  187.1 1.3 collective-permute-done.18
  188.4 2.0 collective-permute-done.16
  190.5 4.2 %collective-permute-start.20 = (f32[48,576]{1,0:T(8,128)S(1)}, f32[48,576]{1,0:T(8,128)S(1)}, u32[]{:S(2)}, u32[]{:S(2)}) collective-permute-start(f32[48,576]{1,0:T(8,128)S(1)} %pad_maximum_fusion), channel_id=1, source_target_pairs={{0,128},{32,160},{64,192},{96,224},{128,0},{160,32},{192,64},{224,... | collective-permute-start | bytes 331784 | tf_op jit(solution)/shard_map/ppermute | solution.py:53
  195.1 2.0 collective-permute-start.19
  197.1 1.3 collective-permute-done.20
  198.4 9.3 %collective-permute-done.21 = f32[48,576]{1,0:T(8,128)S(1)} collective-permute-done((f32[48,576]{1,0:T(8,128)S(1)}, f32[48,576]{1,0:T(8,128)S(1)}, u32[]{:S(2)}, u32[]{:S(2)}) %collective-permute-start.21) | collective-permute-done | bytes 110624 | tf_op jit(solution)/shard_map/ppermute | solution.py:53
  208.8 1.4 collective-permute-start.23
  210.5 2.6 %collective-permute-done.24 = f32[48,576]{1,0:T(8,128)S(1)} collective-permute-done((f32[48,576]{1,0:T(8,128)S(1)}, f32[48,576]{1,0:T(8,128)S(1)}, u32[]{:S(2)}, u32[]{:S(2)}) %collective-permute-start.24) | collective-permute-done | bytes 110624 | tf_op jit(solution)/shard_map/ppermute | solution.py:48
  213.1 2.7 %collective-permute-done.23 = f32[48,576]{1,0:T(8,128)S(1)} collective-permute-done((f32[48,576]{1,0:T(8,128)S(1)}, f32[48,576]{1,0:T(8,128)S(1)}, u32[]{:S(2)}, u32[]{:S(2)}) %collective-permute-start.23) | collective-permute-done | bytes 110624 | tf_op jit(solution)/shard_map/ppermute | solution.py:48
  216.2 1.3 collective-permute-start.25
  217.5 1.4 collective-permute-done.25.other_ref
  218.9 1.7 shard_map.119
  (66 shorter events, 13.5 us)
Async XLA Ops:
  0.7 1.2 copy-start.3
  1.9 0.7 copy-start.8
  2.6 0.7 copy-start.9
  4.3 4.7 %collective-permute-start = (f32[48,2304]{1,0:T(8,128)S(1)}, f32[48,2304]{1,0:T(8,128)S(1)}, u32[]{:S(2)}, u32[]{:S(2)}) collective-permute-start(f32[48,2304]{1,0:T(8,128)S(1)} %get-tuple-element.20), channel_id=1, source_target_pairs={{0,8},{8,0},{1,9},{9,1},{2,10},{10,2},{3,11},{11,3},{4,12},{12,4},... | collective-permute-start | bytes 1327112 | tf_op jit(solution)/shard_map/ppermute | solution.py:38
  9.2 5.5 %collective-permute-start.3 = (f32[48,576]{1,0:T(8,128)S(1)}, f32[48,576]{1,0:T(8,128)S(1)}, u32[]{:S(2)}, u32[]{:S(2)}) collective-permute-start(f32[48,576]{1,0:T(8,128)S(1)} %select_select_fusion.8), channel_id=1, source_target_pairs={{0,48},{16,32},{32,16},{48,0},{64,112},{80,96},{96,80},{112,64},{1... | collective-permute-start | bytes 331784 | tf_op jit(solution)/shard_map/ppermute | solution.py:48
  10.2 7.8 %collective-permute-start.1 = (f32[48,576]{1,0:T(8,128)S(1)}, f32[48,576]{1,0:T(8,128)S(1)}, u32[]{:S(2)}, u32[]{:S(2)}) collective-permute-start(f32[48,576]{1,0:T(8,128)S(1)} %get-tuple-element.42), channel_id=1, source_target_pairs={{0,16},{16,0},{32,48},{48,32},{64,80},{80,64},{96,112},{112,96},{1... | collective-permute-start | bytes 331784 | tf_op jit(solution)/shard_map/ppermute | solution.py:48
  10.6 7.5 %collective-permute-start.2 = (f32[48,576]{1,0:T(8,128)S(1)}, f32[48,576]{1,0:T(8,128)S(1)}, u32[]{:S(2)}, u32[]{:S(2)}) collective-permute-start(f32[48,576]{1,0:T(8,128)S(1)} %get-tuple-element.43), channel_id=1, source_target_pairs={{0,32},{16,48},{32,0},{48,16},{64,96},{80,112},{96,64},{112,80},{1... | collective-permute-start | bytes 331784 | tf_op jit(solution)/shard_map/ppermute | solution.py:48
  12.2 34.3 %copy-start.6 = (f32[12,384]{1,0:T(8,128)S(1)}, f32[12,384]{1,0:T(8,128)}, u32[]{:S(2)}) copy-start(f32[12,384]{1,0:T(8,128)} %constant.144.clone.sin_ref) | copy-start | bytes 55300
  12.2 34.3 %copy-start.7 = (f32[12,384]{1,0:T(8,128)S(1)}, f32[12,384]{1,0:T(8,128)}, u32[]{:S(2)}) copy-start(f32[12,384]{1,0:T(8,128)} %constant.143.clone.cos_ref) | copy-start | bytes 55300
  12.2 34.3 %copy-start.10 = (bf16[768,768]{1,0:T(8,128)(2,1)S(1)}, bf16[768,768]{1,0:T(8,128)(2,1)}, u32[]{:S(2)}) copy-start(bf16[768,768]{1,0:T(8,128)(2,1)} %constant.146.clone.low_source) | copy-start | bytes 3538948
  18.2 8.6 %collective-permute-start.6 = (f32[48,576]{1,0:T(8,128)S(1)}, f32[48,576]{1,0:T(8,128)S(1)}, u32[]{:S(2)}, u32[]{:S(2)}) collective-permute-start(f32[48,576]{1,0:T(8,128)S(1)} %add_add_fusion.2), channel_id=1, source_target_pairs={{0,192},{32,224},{64,0},{96,32},{128,64},{160,96},{192,128},{224,1... | collective-permute-start | bytes 331784 | tf_op jit(solution)/shard_map/ppermute | solution.py:53
  22.6 11.1 %collective-permute-start.5 = (f32[48,576]{1,0:T(8,128)S(1)}, f32[48,576]{1,0:T(8,128)S(1)}, u32[]{:S(2)}, u32[]{:S(2)}) collective-permute-start(f32[48,576]{1,0:T(8,128)S(1)} %add_add_fusion.2), channel_id=1, source_target_pairs={{0,128},{32,160},{64,192},{96,224},{128,0},{160,32},{192,64},{224,... | collective-permute-start | bytes 331784 | tf_op jit(solution)/shard_map/ppermute | solution.py:53
  23.6 10.1 %collective-permute-start.4 = (f32[48,576]{1,0:T(8,128)S(1)}, f32[48,576]{1,0:T(8,128)S(1)}, u32[]{:S(2)}, u32[]{:S(2)}) collective-permute-start(f32[48,576]{1,0:T(8,128)S(1)} %add_add_fusion.2), channel_id=1, source_target_pairs={{0,64},{32,96},{64,128},{96,160},{128,192},{160,224},{192,0},{224,... | collective-permute-start | bytes 331784 | tf_op jit(solution)/shard_map/ppermute | solution.py:53
  33.7 6.2 %collective-permute-start.9 = (f32[48,576]{1,0:T(8,128)S(1)}, f32[48,576]{1,0:T(8,128)S(1)}, u32[]{:S(2)}, u32[]{:S(2)}) collective-permute-start(f32[48,576]{1,0:T(8,128)S(1)} %add_add_fusion.1), channel_id=1, source_target_pairs={{0,48},{16,32},{32,16},{48,0},{64,112},{80,96},{96,80},{112,64},{1... | collective-permute-start | bytes 331784 | tf_op jit(solution)/shard_map/ppermute | solution.py:48
  37.6 5.0 %collective-permute-start.8 = (f32[48,576]{1,0:T(8,128)S(1)}, f32[48,576]{1,0:T(8,128)S(1)}, u32[]{:S(2)}, u32[]{:S(2)}) collective-permute-start(f32[48,576]{1,0:T(8,128)S(1)} %add_add_fusion.1), channel_id=1, source_target_pairs={{0,32},{16,48},{32,0},{48,16},{64,96},{80,112},{96,64},{112,80},{1... | collective-permute-start | bytes 331784 | tf_op jit(solution)/shard_map/ppermute | solution.py:48
  37.6 5.3 %collective-permute-start.7 = (f32[48,576]{1,0:T(8,128)S(1)}, f32[48,576]{1,0:T(8,128)S(1)}, u32[]{:S(2)}, u32[]{:S(2)}) collective-permute-start(f32[48,576]{1,0:T(8,128)S(1)} %add_add_fusion.1), channel_id=1, source_target_pairs={{0,16},{16,0},{32,48},{48,32},{64,80},{80,64},{96,112},{112,96},{1... | collective-permute-start | bytes 331784 | tf_op jit(solution)/shard_map/ppermute | solution.py:48
  43.2 3.2 %collective-permute-start.10 = (f32[48,2304]{1,0:T(8,128)S(1)}, f32[48,2304]{1,0:T(8,128)S(1)}, u32[]{:S(2)}, u32[]{:S(2)}) collective-permute-start(f32[48,2304]{1,0:T(8,128)S(1)} %concatenate.9.half_ref), channel_id=1, source_target_pairs={{0,8},{8,0},{1,9},{9,1},{2,10},{10,2},{3,11},{11,3},{4,12},{12,4},... | collective-permute-start | bytes 1327112 | tf_op jit(solution)/shard_map/ppermute | solution.py:38
  46.4 1.3 copy-start.11
  57.7 1.3 copy-start
  59.0 48.4 %copy-start.12 = (bf16[384,576]{1,0:T(8,128)(2,1)S(1)}, bf16[384,576]{1,0:T(8,128)(2,1)}, u32[]{:S(2)}) copy-start(bf16[384,576]{1,0:T(8,128)(2,1)} %constant.147.clone.table_ref) | copy-start | bytes 1327108
  59.0 48.4 %all-to-all-start = ((f32[8,96,1152]{2,1,0:T(8,128)}), f32[8,96,1152]{2,1,0:T(8,128)}, u32[]{:S(2)}, u32[]{:S(2)}) async-start(f32[8,96,1152]{2,1,0:T(8,128)} %get-tuple-element.22), calls=%async_computation | async-start | bytes 7077888 | tf_op jit(solution)/shard_map/all_to_all | solution.py:479
  115.9 27.9 %all-to-all-start.2 = ((f32[8,48,1152]{2,1,0:T(8,128)}), f32[8,48,1152]{2,1,0:T(8,128)}, u32[]{:S(2)}, u32[]{:S(2)}) async-start(f32[8,48,1152]{2,1,0:T(8,128)} %shard_map.116), calls=%async_computation.2 | async-start | bytes 3538944 | tf_op jit(solution)/shard_map/all_to_all | solution.py:479
  129.5 19.5 %copy-start.1 = (bf16[768,768]{1,0:T(8,128)(2,1)S(1)}, bf16[768,768]{1,0:T(8,128)(2,1)}, u32[]{:S(2)}) copy-start(bf16[768,768]{1,0:T(8,128)(2,1)} %constant.149.clone.low_source) | copy-start | bytes 3538948
  129.5 19.5 %copy-start.2 = (bf16[768,768]{1,0:T(8,128)(2,1)S(1)}, bf16[768,768]{1,0:T(8,128)(2,1)}, u32[]{:S(2)}) copy-start(bf16[768,768]{1,0:T(8,128)(2,1)} %constant.148.clone.high_source) | copy-start | bytes 3538948
  143.9 28.7 %all-to-all-start.1 = ((f32[8,48,1152]{2,1,0:T(8,128)}), f32[8,48,1152]{2,1,0:T(8,128)}, u32[]{:S(2)}, u32[]{:S(2)}) async-start(f32[8,48,1152]{2,1,0:T(8,128)} %shard_map.115), calls=%async_computation.1 | async-start | bytes 3538944 | tf_op jit(solution)/shard_map/all_to_all | solution.py:479
  154.8 0.9 copy-start.4
  155.7 1.9 collective-permute-start.11
  157.7 4.7 %collective-permute-start.14 = (f32[24,576]{1,0:T(8,128)S(1)}, f32[24,576]{1,0:T(8,128)S(1)}, u32[]{:S(2)}, u32[]{:S(2)}) collective-permute-start(f32[24,576]{1,0:T(8,128)S(1)} %select_select_fusion.14), channel_id=1, source_target_pairs={{0,48},{16,32},{32,16},{48,0},{64,112},{80,96},{96,80},{112,64},{1... | collective-permute-start | bytes 165896 | tf_op jit(solution)/shard_map/ppermute | solution.py:48
  159.5 11.9 %collective-permute-start.12 = (f32[24,576]{1,0:T(8,128)S(1)}, f32[24,576]{1,0:T(8,128)S(1)}, u32[]{:S(2)}, u32[]{:S(2)}) collective-permute-start(f32[24,576]{1,0:T(8,128)S(1)} %get-tuple-element.46), channel_id=1, source_target_pairs={{0,16},{16,0},{32,48},{48,32},{64,80},{80,64},{96,112},{112,96},{1... | collective-permute-start | bytes 165896 | tf_op jit(solution)/shard_map/ppermute | solution.py:48
  160.8 10.6 %collective-permute-start.13 = (f32[24,576]{1,0:T(8,128)S(1)}, f32[24,576]{1,0:T(8,128)S(1)}, u32[]{:S(2)}, u32[]{:S(2)}) collective-permute-start(f32[24,576]{1,0:T(8,128)S(1)} %get-tuple-element.47), channel_id=1, source_target_pairs={{0,32},{16,48},{32,0},{48,16},{64,96},{80,112},{96,64},{112,80},{1... | collective-permute-start | bytes 165896 | tf_op jit(solution)/shard_map/ppermute | solution.py:48
  172.6 1.2 copy-start.5
  180.6 3.5 %collective-permute-start.15 = (f32[24,2304]{1,0:T(8,128)S(1)}, f32[24,2304]{1,0:T(8,128)S(1)}, u32[]{:S(2)}, u32[]{:S(2)}) collective-permute-start(f32[24,2304]{1,0:T(8,128)S(1)} %get-tuple-element.33), channel_id=1, source_target_pairs={{0,8},{8,0},{1,9},{9,1},{2,10},{10,2},{3,11},{11,3},{4,12},{12,4},... | collective-permute-start | bytes 663560 | tf_op jit(solution)/shard_map/ppermute | solution.py:38
  184.4 4.1 %collective-permute-start.18 = (f32[24,576]{1,0:T(8,128)S(1)}, f32[24,576]{1,0:T(8,128)S(1)}, u32[]{:S(2)}, u32[]{:S(2)}) collective-permute-start(f32[24,576]{1,0:T(8,128)S(1)} %select_select_fusion.11), channel_id=1, source_target_pairs={{0,48},{16,32},{32,16},{48,0},{64,112},{80,96},{96,80},{112,64},{1... | collective-permute-start | bytes 165896 | tf_op jit(solution)/shard_map/ppermute | solution.py:48
  185.8 4.6 %collective-permute-start.16 = (f32[24,576]{1,0:T(8,128)S(1)}, f32[24,576]{1,0:T(8,128)S(1)}, u32[]{:S(2)}, u32[]{:S(2)}) collective-permute-start(f32[24,576]{1,0:T(8,128)S(1)} %get-tuple-element.44), channel_id=1, source_target_pairs={{0,16},{16,0},{32,48},{48,32},{64,80},{80,64},{96,112},{112,96},{1... | collective-permute-start | bytes 165896 | tf_op jit(solution)/shard_map/ppermute | solution.py:48
  187.0 3.4 %collective-permute-start.17 = (f32[24,576]{1,0:T(8,128)S(1)}, f32[24,576]{1,0:T(8,128)S(1)}, u32[]{:S(2)}, u32[]{:S(2)}) collective-permute-start(f32[24,576]{1,0:T(8,128)S(1)} %get-tuple-element.45), channel_id=1, source_target_pairs={{0,32},{16,48},{32,0},{48,16},{64,96},{80,112},{96,64},{112,80},{1... | collective-permute-start | bytes 165896 | tf_op jit(solution)/shard_map/ppermute | solution.py:48
  190.5 7.8 %collective-permute-start.20 = (f32[48,576]{1,0:T(8,128)S(1)}, f32[48,576]{1,0:T(8,128)S(1)}, u32[]{:S(2)}, u32[]{:S(2)}) collective-permute-start(f32[48,576]{1,0:T(8,128)S(1)} %pad_maximum_fusion), channel_id=1, source_target_pairs={{0,128},{32,160},{64,192},{96,224},{128,0},{160,32},{192,64},{224,... | collective-permute-start | bytes 331784 | tf_op jit(solution)/shard_map/ppermute | solution.py:53
  194.8 13.0 %collective-permute-start.21 = (f32[48,576]{1,0:T(8,128)S(1)}, f32[48,576]{1,0:T(8,128)S(1)}, u32[]{:S(2)}, u32[]{:S(2)}) collective-permute-start(f32[48,576]{1,0:T(8,128)S(1)} %pad_maximum_fusion), channel_id=1, source_target_pairs={{0,192},{32,224},{64,0},{96,32},{128,64},{160,96},{192,128},{224,1... | collective-permute-start | bytes 331784 | tf_op jit(solution)/shard_map/ppermute | solution.py:53
  195.1 12.6 %collective-permute-start.19 = (f32[48,576]{1,0:T(8,128)S(1)}, f32[48,576]{1,0:T(8,128)S(1)}, u32[]{:S(2)}, u32[]{:S(2)}) collective-permute-start(f32[48,576]{1,0:T(8,128)S(1)} %pad_maximum_fusion), channel_id=1, source_target_pairs={{0,64},{32,96},{64,128},{96,160},{128,192},{160,224},{192,0},{224,... | collective-permute-start | bytes 331784 | tf_op jit(solution)/shard_map/ppermute | solution.py:53
  207.8 5.3 %collective-permute-start.24 = (f32[48,576]{1,0:T(8,128)S(1)}, f32[48,576]{1,0:T(8,128)S(1)}, u32[]{:S(2)}, u32[]{:S(2)}) collective-permute-start(f32[48,576]{1,0:T(8,128)S(1)} %add_add_fusion), channel_id=1, source_target_pairs={{0,48},{16,32},{32,16},{48,0},{64,112},{80,96},{96,80},{112,64},{1... | collective-permute-start | bytes 331784 | tf_op jit(solution)/shard_map/ppermute | solution.py:48
  208.8 7.0 %collective-permute-start.23 = (f32[48,576]{1,0:T(8,128)S(1)}, f32[48,576]{1,0:T(8,128)S(1)}, u32[]{:S(2)}, u32[]{:S(2)}) collective-permute-start(f32[48,576]{1,0:T(8,128)S(1)} %add_add_fusion), channel_id=1, source_target_pairs={{0,32},{16,48},{32,0},{48,16},{64,96},{80,112},{96,64},{112,80},{1... | collective-permute-start | bytes 331784 | tf_op jit(solution)/shard_map/ppermute | solution.py:48
  210.2 5.7 %collective-permute-start.22 = (f32[48,576]{1,0:T(8,128)S(1)}, f32[48,576]{1,0:T(8,128)S(1)}, u32[]{:S(2)}, u32[]{:S(2)}) collective-permute-start(f32[48,576]{1,0:T(8,128)S(1)} %add_add_fusion), channel_id=1, source_target_pairs={{0,16},{16,0},{32,48},{48,32},{64,80},{80,64},{96,112},{112,96},{1... | collective-permute-start | bytes 331784 | tf_op jit(solution)/shard_map/ppermute | solution.py:48
  216.2 2.7 %collective-permute-start.25 = (f32[48,2304]{1,0:T(8,128)S(1)}, f32[48,2304]{1,0:T(8,128)S(1)}, u32[]{:S(2)}, u32[]{:S(2)}) collective-permute-start(f32[48,2304]{1,0:T(8,128)S(1)} %concatenate.11.own_ref), channel_id=1, source_target_pairs={{0,8},{8,0},{1,9},{9,1},{2,10},{10,2},{3,11},{11,3},{4,12},{12,4},... | collective-permute-start | bytes 1327112 | tf_op jit(solution)/shard_map/ppermute | solution.py:38

commit v2 on v1

--- a/solution.py
+++ b/solution.py
@@ -188,10 +188,16 @@
     return result
 
 
-def forward_kernel(
-    here_ref, orbital_ref, half_ref, other_ref, cos_ref, sin_ref, high_source, low_source,
-    out_ref, chosen_ref, field, field_high, field_low, high_ref, low_ref, loaded,
-):
+def spot_of(here_ref, piece, direction):
+    return (here_ref[2] ^ (piece // 4)) * 4 + (here_ref[3] + direction * (piece % 4)) % 4
+
+
+def forward_kernel(step, whole, here_ref, orbital_ref, half_ref, other_ref, cos_ref, sin_ref, high_source, low_source, *rest):
+    count = 1 if whole else SLABS
+    outs, chosen_ref = rest[:count], rest[count]
+    field, field_high, field_low, staged, high_ref, low_ref, loaded = rest[count + 1 :]
+    if whole:
+        staged = outs[0]
     loads = [
         pltpu.make_async_copy(source, target, loaded.at[index])
         for index, (source, target) in enumerate(((high_source, high_ref), (low_source, low_ref)))
@@ -199,57 +205,63 @@
     for load in loads:
         load.start()
     core = here_ref[1]
-    for step in range(STEPS):
-        for offset in range(0, MIDDLE, LANES):
-            for where, source in ((core, half_ref), (1 - core, other_ref)):
-                lanes = pl.ds(pl.multiple_of(where * MIDDLE + offset, 128), LANES)
-                for a in range(2):
-                    first = (step * 2 + a) * PLANES
-                    rows = source[first : first + PLANES, offset : offset + LANES]
-                    chosen_ref[step, a, :, lanes] = jnp.concatenate([rows, rows], axis=0)
-
-    for step in range(STEPS):
-
-        def tile(index, carry):
-            for group in range(2):
-                for part in range(3):
-                    rows = pl.ds(pl.multiple_of(group * PAIR + index * 8, 8), 8)
-                    own = pl.ds(pl.multiple_of(index * 8, 8), 8)
-                    values = []
-                    for block in range(BLOCKS):
-                        lanes = pl.ds(block * LANES + part * 128, 128)
-                        orbital = orbital_ref[rows, lanes]
-                        values.append(
-                            (orbital * chosen_ref[step, 0, own, lanes], orbital * chosen_ref[step, 1, own, lanes])
-                        )
-                    values = dft12(values, -1)
-                    for kb, (re, im) in enumerate(values):
-                        cosine = cos_ref[kb : kb + 1, part * 128 : part * 128 + 128]
-                        sine = sin_ref[kb : kb + 1, part * 128 : part * 128 + 128]
-                        to = pl.ds(pl.multiple_of(kb * ROWS + group * PAIR + index * 8, 8), 8)
-                        field[to, pl.ds(part * 128, 128)] = re * cosine - im * sine
-                        field[to, pl.ds(LANES + part * 128, 128)] = re * sine + im * cosine
-            return carry
-
-        lax.fori_loop(0, PAIR // 8, tile, 0)
-        field_high[...], field_low[...] = split(field[...])
-        if step == 0:
-            for load in loads:
-                load.wait()
-        for piece in range(3):
-            lanes = pl.ds(piece * 256, 256)
-            high = high_ref[:, lanes]
-            result = dot(field_high[...], high) + dot(field_low[...], high) + dot(field_high[...], low_ref[:, lanes])
-            for part in range(2):
-                half, offset = divmod(2 * piece + part, 3)
-                for kb in range(BLOCKS):
-                    column, turn = divmod(kb, 3)
-                    out_ref[
-                        half * 4 + column, pl.ds(step * ROWS, ROWS), pl.ds(turn * LANES + offset * 128, 128)
-                    ] = result[kb * ROWS : kb * ROWS + ROWS, part * 128 : part * 128 + 128]
-
-
-def middle_kernel(step, value_ref, kernel_ref, table_ref, out_ref):
+    for offset in range(0, MIDDLE, LANES):
+        for where, source in ((core, half_ref), (1 - core, other_ref)):
+            lanes = pl.ds(pl.multiple_of(where * MIDDLE + offset, 128), LANES)
+            for a in range(2):
+                first = (step * 2 + a) * PLANES
+                rows = source[first : first + PLANES, offset : offset + LANES]
+                chosen_ref[a, :, lanes] = jnp.concatenate([rows, rows], axis=0)
+
+
+    def tile(index, carry):
+        for group in range(2):
+            for part in range(3):
+                rows = pl.ds(pl.multiple_of(group * PAIR + index * 8, 8), 8)
+                own = pl.ds(pl.multiple_of(index * 8, 8), 8)
+                values = []
+                for block in range(BLOCKS):
+                    lanes = pl.ds(block * LANES + part * 128, 128)
+                    orbital = orbital_ref[rows, lanes]
+                    values.append(
+                        (orbital * chosen_ref[0, own, lanes], orbital * chosen_ref[1, own, lanes])
+                    )
+                values = dft12(values, -1)
+                for kb, (re, im) in enumerate(values):
+                    cosine = cos_ref[kb : kb + 1, part * 128 : part * 128 + 128]
+                    sine = sin_ref[kb : kb + 1, part * 128 : part * 128 + 128]
+                    to = pl.ds(pl.multiple_of(kb * ROWS + group * PAIR + index * 8, 8), 8)
+                    field[to, pl.ds(part * 128, 128)] = re * cosine - im * sine
+                    field[to, pl.ds(LANES + part * 128, 128)] = re * sine + im * cosine
+        return carry
+
+    lax.fori_loop(0, PAIR // 8, tile, 0)
+    field_high[...], field_low[...] = split(field[...])
+    for load in loads:
+        load.wait()
+    for piece in range(3):
+        lanes = pl.ds(piece * 256, 256)
+        high = high_ref[:, lanes]
+        result = dot(field_high[...], high) + dot(field_low[...], high) + dot(field_high[...], low_ref[:, lanes])
+        for part in range(2):
+            half, offset = divmod(2 * piece + part, 3)
+            for kb in range(BLOCKS):
+                column, turn = divmod(kb, 3)
+                staged[
+                    half * 4 + column, :, pl.ds(turn * LANES + offset * 128, 128)
+                ] = result[kb * ROWS : kb * ROWS + ROWS, part * 128 : part * 128 + 128]
+    for piece, out_ref in enumerate(() if whole else outs):
+        out_ref[...] = staged[spot_of(here_ref, piece, 1)]
+
+
+def middle_kernel(whole, here_ref, *refs):
+    count = 1 if whole else SLABS
+    values, kernel_ref, table_ref = refs[:count], refs[count], refs[count + 1]
+    outs, staged = refs[count + 2 : -1], refs[-1]
+    source = values[0] if whole else staged
+    target = outs[0] if whole else staged
+    for piece, value_ref in enumerate(() if whole else values):
+        staged[spot_of(here_ref, piece, -1)] = value_ref[...]
     imaginary = lax.broadcasted_iota(jnp.int32, (2 * NZ, LANES), 1) >= HALF
 
     def swapped(x):
@@ -262,35 +274,42 @@
         return cosine + jnp.where(imaginary, -sign * sine, sign * sine)
 
     for group in range(ROWS // PAIR):
-        source = slice(step * ROWS + group * PAIR, step * ROWS + group * PAIR + PAIR)
         own = slice(group * PAIR, group * PAIR + PAIR)
         for turn in range(3):
             lanes = slice(turn * LANES, turn * LANES + LANES)
-            x = jnp.concatenate([value_ref[slab, source, lanes] for slab in range(SLABS)], axis=0)
+            x = jnp.concatenate([source[slab, own, lanes] for slab in range(SLABS)], axis=0)
             x = transform(x, 1.0) * kernel_ref[:, lanes]
             x = transform(x, -1.0)
             for slab in range(SLABS):
-                out_ref[slab, own, lanes] = x[slab * PAIR : slab * PAIR + PAIR]
+                target[slab, own, lanes] = x[slab * PAIR : slab * PAIR + PAIR]
+    for piece, out_ref in enumerate(() if whole else outs):
+        out_ref[...] = staged[spot_of(here_ref, piece, 1)]
 
 
 def inverse_kernel(
-    step, here_ref, value_ref, orbital_ref, chosen_ref, cos_ref, sin_ref, high_source, low_source, *rest
+    step, whole, here_ref, orbital_ref, chosen_ref, cos_ref, sin_ref, high_source, low_source, *rest
 ):
+    count = 1 if whole else SLABS
+    values, rest = rest[:count], rest[count:]
     if step == 0:
-        applied_ref, kept_ref, sent_ref, field_high, field_low, field, totals, high_ref, low_ref, loaded = rest
+        applied_ref, kept_ref, sent_ref, field_high, field_low, field, totals, staged, high_ref, low_ref, loaded = rest
         sums = applied_ref
     else:
-        before_ref, applied_ref, kept_ref, sent_ref, field_high, field_low, field, totals, high_ref, low_ref, loaded, sums = rest
+        before_ref, applied_ref, kept_ref, sent_ref, field_high, field_low, field, totals, staged, high_ref, low_ref, loaded, sums = rest
     loads = [
         pltpu.make_async_copy(source, target, loaded.at[index])
         for index, (source, target) in enumerate(((high_source, high_ref), (low_source, low_ref)))
     ]
     for load in loads:
         load.start()
+    if whole:
+        staged = values[0]
+    for piece, value_ref in enumerate(() if whole else values):
+        staged[spot_of(here_ref, piece, -1)] = value_ref[...]
     for kb in range(BLOCKS):
         column, turn = divmod(kb, 3)
         for half in range(2):
-            x = value_ref[half * 4 + column, :, pl.ds(turn * LANES, LANES)]
+            x = staged[half * 4 + column, :, pl.ds(turn * LANES, LANES)]
             high, low = split(x)
             field_high[kb * ROWS : kb * ROWS + ROWS, half * LANES : half * LANES + LANES] = high
             field_low[kb * ROWS : kb * ROWS + ROWS, half * LANES : half * LANES + LANES] = low
@@ -320,7 +339,7 @@
                 for block, (first, second) in enumerate(values):
                     lanes = pl.ds(block * LANES + part * 128, 128)
                     orbital = orbital_ref[rows, lanes]
-                    applied = first * chosen_ref[step, 0, own, lanes] + second * chosen_ref[step, 1, own, lanes]
+                    applied = first * chosen_ref[0, own, lanes] + second * chosen_ref[1, own, lanes]
                     if step == 0:
                         sums[rows, lanes] = applied
                     else:
@@ -418,38 +437,46 @@
 ]
 
 
-def to_columns(here, orbitals, half, other):
+PIECE = jax.ShapeDtypeStruct((ROWS, COLUMNS), jnp.float32)
+WHOLE = jax.ShapeDtypeStruct((SLABS, ROWS, COLUMNS), jnp.float32)
+STAGED = pltpu.VMEM((SLABS, ROWS, COLUMNS), jnp.float32)
+
+
+def to_columns(here, orbitals, half, other, step, whole):
+    shapes = (WHOLE,) if whole else (PIECE,) * SLABS
     forward, _, twiddle, _ = tables()
     tall = BLOCKS * ROWS
-    return pl.pallas_call(
-        forward_kernel,
-        out_shape=(
-            jax.ShapeDtypeStruct((SLABS, STEPS * ROWS, COLUMNS), jnp.float32),
-            jax.ShapeDtypeStruct((STEPS, 2, PAIR, POINTS), jnp.float32),
-        ),
+    *columns, chosen = pl.pallas_call(
+        functools.partial(forward_kernel, step, whole),
+        out_shape=shapes + (jax.ShapeDtypeStruct((2, PAIR, POINTS), jnp.float32),),
         in_specs=[SMEM] + [VMEM] * 5 + [HBM] * 2,
-        out_specs=(VMEM, VMEM),
+        out_specs=(VMEM,) * (len(shapes) + 1),
         scratch_shapes=[
             pltpu.VMEM((tall, 2 * LANES), jnp.float32),
             pltpu.VMEM((tall, 2 * LANES), jnp.bfloat16),
             pltpu.VMEM((tall, 2 * LANES), jnp.bfloat16),
+            STAGED,
         ]
         + TABLE_SCRATCH,
-        cost_estimate=cost(12 * tall * (2 * LANES) ** 2, 4_000_000),
+        cost_estimate=cost(6 * tall * (2 * LANES) ** 2, 4_000_000),
         **PARAMS,
     )(here, orbitals, half, other, *twiddle, *forward)
-
-
-def screened(values, kernel, step):
+    return columns, chosen
+
+
+def screened(here, values, kernel):
     _, _, _, along_z = tables()
+    whole = len(values) == 1
+    shapes = (WHOLE,) if whole else (PIECE,) * SLABS
     return pl.pallas_call(
-        functools.partial(middle_kernel, step),
-        out_shape=jax.ShapeDtypeStruct((SLABS, ROWS, COLUMNS), jnp.float32),
-        in_specs=[VMEM] * 3,
-        out_specs=VMEM,
+        functools.partial(middle_kernel, whole),
+        out_shape=shapes,
+        in_specs=[SMEM] + [VMEM] * (len(values) + 2),
+        out_specs=(VMEM,) * len(shapes),
+        scratch_shapes=[STAGED],
         cost_estimate=cost(2 * 4 * 4 * NZ * 6 * NZ * COLUMNS, 4_000_000),
         **PARAMS,
-    )(values, kernel, along_z)
+    )(here, *values, kernel, along_z)
 
 
 def from_columns(here, values, orbitals, chosen, step, before=None):
@@ -458,43 +485,56 @@
     first_step = before is None
     applied = (ROWS, POINTS) if first_step else (PLANES, BLOC, POINTS)
     return pl.pallas_call(
-        functools.partial(inverse_kernel, step),
+        functools.partial(inverse_kernel, step, len(values) == 1),
         out_shape=(jax.ShapeDtypeStruct(applied, jnp.float32), HALF_SHAPE, HALF_SHAPE),
-        in_specs=[SMEM] + [VMEM] * 5 + [HBM] * 2 + ([] if first_step else [VMEM]),
+        in_specs=[SMEM] + [VMEM] * 4 + [HBM] * 2 + [VMEM] * (len(values) + (0 if first_step else 1)),
         out_specs=(VMEM,) * 3,
         scratch_shapes=[
             pltpu.VMEM((tall, 2 * LANES), jnp.bfloat16),
             pltpu.VMEM((tall, 2 * LANES), jnp.bfloat16),
             pltpu.VMEM((tall, 2 * LANES), jnp.float32),
             pltpu.VMEM((2, PAIR, POINTS), jnp.float32),
+            STAGED,
         ]
         + TABLE_SCRATCH
         + ([] if first_step else [pltpu.VMEM((ROWS, POINTS), jnp.float32)]),
         cost_estimate=cost(6 * tall * (2 * LANES) ** 2, 8_000_000),
         **PARAMS,
-    )(here, values, orbitals, chosen, *twiddle, *inverse, *(() if first_step else (before,)))
-
-
-def exchange(columns):
-    return lax.all_to_all(columns, ("xh", "y"), split_axis=0, concat_axis=0, tiled=True)
+    )(here, orbitals, chosen, *twiddle, *inverse, *values, *(() if first_step else (before,)))
+
+
+def exchange(pieces):
+    if len(pieces) == 1:
+        return [lax.all_to_all(pieces[0], ("xh", "y"), split_axis=0, concat_axis=0, tiled=True)]
+    moved = [pieces[0]]
+    for piece in range(1, SLABS):
+        pairs = [
+            (x * 4 + y, (x ^ (piece // 4)) * 4 + (y + piece % 4) % 4) for x in range(2) for y in range(4)
+        ]
+        moved.append(lax.ppermute(pieces[piece], ("xh", "y"), pairs))
+    return moved
 
 
 def per_device(orbitals, owner, picks):
-    core = lax.axis_index("c")
+    core, xh, y = lax.axis_index("c"), lax.axis_index("xh"), lax.axis_index("y")
     group = (lax.axis_index("z") * 2 + lax.axis_index("xl")) * 2 + core
-    here = jnp.stack([group, core]).astype(jnp.int32)
+    here = jnp.stack([group, core, xh, y]).astype(jnp.int32)
     flat, kept, sent = pick_orbitals(here, owner, picks, orbitals.transpose(1, 0, 2))
     half = spread_near(join_far(join_near(join_cores(kept, sent))))
     other = swap(half, "c", 1)
-    columns, chosen = to_columns(here, flat, half, other)
-    columns, xh, y = tie(columns, lax.axis_index("xh"), lax.axis_index("y"))
+    columns0, chosen0 = to_columns(here, flat, half, other, 0, True)
+    forward0 = exchange(columns0)
+    half, _ = tie(half, chosen0)
+    columns1, chosen1 = to_columns(here, flat, half, other, 1, True)
+    first, xh, y = tie(columns1[0], xh, y)
     kernel = kernel_columns(xh, y)
-    forward = exchange(columns)
-    backward = [exchange(screened(forward, kernel, step)) for step in range(STEPS)]
-    applied, kept, sent = from_columns(here, backward[0], flat, chosen, 0)
+    forward1 = exchange([first] + columns1[1:])
+    backward0 = exchange(screened(here, forward0, kernel))
+    backward1 = exchange(screened(here, forward1, kernel))
+    applied, kept, sent = from_columns(here, backward0, flat, chosen0, 0)
     part = join_near(join_cores(kept, sent))
-    last, part = tie(backward[1], part)
-    applied, kept, sent = from_columns(here, last, flat, chosen, 1, applied)
+    last, part = tie(backward1[0], part)
+    applied, kept, sent = from_columns(here, [last] + backward1[1:], flat, chosen1, 1, applied)
     part = jnp.concatenate([part, join_near(join_cores(kept, sent))], axis=0)
     half = spread_near(join_far(part))
     other = swap(half, "c", 1)

time: 221 us -> 217 us (0.982)
  waiting for transfers between devices: 112 us -> 96.1 us
  local copies, waits for them, and re-layouts: 7.46 us -> 17.6 us
  starting transfers between devices: 56.5 us -> 61.7 us
  Pallas kernels: 42.2 us -> 37.4 us
    all_to_all x3 -> x4, waiting for transfers between devices: 56.5 us -> 41.8 us  [exchange(): lax.all_to_all(pieces[0], ('xh', 'y'), split_axis=0, concat_axis=0, tiled...]
    unnamed x26 -> x58, local copies, waits for them, and re-layouts: 7.14 us -> 17.2 us
    all_to_all x3 -> x4, starting transfers between devices: 17.1 us -> 22.3 us  [exchange(): lax.all_to_all(pieces[0], ('xh', 'y'), split_axis=0, concat_axis=0, tiled...]
    pallas_call x5 -> x6, Pallas kernels: 39.5 us -> 34.8 us  [the longest x2 12.5 us: screened(): pl.pallas_call(functools.partial(middle_kernel, whole), out_shape=shapes,...]
  transfers between devices with their start and end apart: 29 -> 30, of which waited for: 24 -> 25; matrix products, arithmetic and copies ran while one was open for 0% -> 1% of each run, Pallas kernels for 6% -> 11%
where the time goes in v2:
time: 217 us
  waiting for transfers between devices  96.1 us (44%)
  starting transfers between devices  61.7 us (28%)
  Pallas kernels  37.4 us (17%)
  local copies, waits for them, and re-layouts  17.6 us (8%)
  other arithmetic  2.64 us (1%)
    all_to_all x4, waiting for transfers between devices, exchange(): lax.all_to_all(pieces[0], ('xh', 'y'), split_axis=0, concat_axis=0, tiled...  41.8 us
    ppermute x15, waiting for transfers between devices, near(): return lax.ppermute(x, ('z', 'xl'), pairs)  29.5 us
    all_to_all x4, starting transfers between devices, exchange(): lax.all_to_all(pieces[0], ('xh', 'y'), split_axis=0, concat_axis=0, tiled...  22.3 us
    ppermute x6, waiting for transfers between devices, along(): lax.ppermute(x, 'z', [(i, (i + distance) % size) for i in range(size)])  18.4 us
    unnamed x58, local copies, waits for them, and re-layouts  17.2 us
    ppermute x15, starting transfers between devices, near(): return lax.ppermute(x, ('z', 'xl'), pairs)  15.7 us
    ppermute x6, starting transfers between devices, along(): lax.ppermute(x, 'z', [(i, (i + distance) % size) for i in range(size)])  14.2 us
    pallas_call x2, Pallas kernels, screened(): pl.pallas_call(functools.partial(middle_kernel, whole), out_shape=shapes,...  12.5 us
  transfers between devices with their start and end apart: 30, of which 25 were waited for; matrix products, arithmetic and copies ran while one was open for 1% of the time, Pallas kernels for 11%

profile of v2, /device:TPU:1, one launch (start us, length us, event | category | flops | bytes accessed | tf_op | source)
XLA Modules:
  0.0 216.5 jit_solution(13801259266058990807)
XLA Ops:
  4.3 3.3 %collective-permute-start = (f32[48,2304]{1,0:T(8,128)S(1)}, f32[48,2304]{1,0:T(8,128)S(1)}, u32[]{:S(2)}, u32[]{:S(2)}) collective-permute-start(f32[48,2304]{1,0:T(8,128)S(1)} %get-tuple-element.23), channel_id=1, source_target_pairs={{0,8},{8,0},{1,9},{9,1},{2,10},{10,2},{3,11},{11,3},{4,12},{12,4},... | collective-permute-start | bytes 1327112 | tf_op jit(solution)/shard_map/ppermute | solution.py:38
  7.6 1.4 collective-permute-done
  10.6 1.6 collective-permute-start.2
  12.2 2.5 %collective-permute-done.3 = f32[48,576]{1,0:T(8,128)S(1)} collective-permute-done((f32[48,576]{1,0:T(8,128)S(1)}, f32[48,576]{1,0:T(8,128)S(1)}, u32[]{:S(2)}, u32[]{:S(2)}) %collective-permute-start.3) | collective-permute-done | bytes 110624 | tf_op jit(solution)/shard_map/ppermute | solution.py:48
  14.7 3.3 %collective-permute-done.1 = f32[48,576]{1,0:T(8,128)S(1)} collective-permute-done((f32[48,576]{1,0:T(8,128)S(1)}, f32[48,576]{1,0:T(8,128)S(1)}, u32[]{:S(2)}, u32[]{:S(2)}) %collective-permute-start.1) | collective-permute-done | bytes 110624 | tf_op jit(solution)/shard_map/ppermute | solution.py:48
  18.2 4.4 %collective-permute-start.6 = (f32[48,576]{1,0:T(8,128)S(1)}, f32[48,576]{1,0:T(8,128)S(1)}, u32[]{:S(2)}, u32[]{:S(2)}) collective-permute-start(f32[48,576]{1,0:T(8,128)S(1)} %add_add_fusion.2), channel_id=1, source_target_pairs={{0,192},{32,224},{64,0},{96,32},{128,64},{160,96},{192,128},{224,1... | collective-permute-start | bytes 331784 | tf_op jit(solution)/shard_map/ppermute | solution.py:53
  23.6 2.3 %collective-permute-start.4 = (f32[48,576]{1,0:T(8,128)S(1)}, f32[48,576]{1,0:T(8,128)S(1)}, u32[]{:S(2)}, u32[]{:S(2)}) collective-permute-start(f32[48,576]{1,0:T(8,128)S(1)} %add_add_fusion.2), channel_id=1, source_target_pairs={{0,64},{32,96},{64,128},{96,160},{128,192},{160,224},{192,0},{224,... | collective-permute-start | bytes 331784 | tf_op jit(solution)/shard_map/ppermute | solution.py:53
  26.9 6.8 %collective-permute-done.5 = f32[48,576]{1,0:T(8,128)S(1)} collective-permute-done((f32[48,576]{1,0:T(8,128)S(1)}, f32[48,576]{1,0:T(8,128)S(1)}, u32[]{:S(2)}, u32[]{:S(2)}) %collective-permute-start.5) | collective-permute-done | bytes 110624 | tf_op jit(solution)/shard_map/ppermute | solution.py:53
  33.7 4.0 %collective-permute-start.9 = (f32[48,576]{1,0:T(8,128)S(1)}, f32[48,576]{1,0:T(8,128)S(1)}, u32[]{:S(2)}, u32[]{:S(2)}) collective-permute-start(f32[48,576]{1,0:T(8,128)S(1)} %add_add_fusion.1), channel_id=1, source_target_pairs={{0,48},{16,32},{32,16},{48,0},{64,112},{80,96},{96,80},{112,64},{1... | collective-permute-start | bytes 331784 | tf_op jit(solution)/shard_map/ppermute | solution.py:48
  38.0 1.9 collective-permute-done.9
  39.9 2.7 %collective-permute-done.8 = f32[48,576]{1,0:T(8,128)S(1)} collective-permute-done((f32[48,576]{1,0:T(8,128)S(1)}, f32[48,576]{1,0:T(8,128)S(1)}, u32[]{:S(2)}, u32[]{:S(2)}) %collective-permute-start.8) | collective-permute-done | bytes 110624 | tf_op jit(solution)/shard_map/ppermute | solution.py:48
  43.2 1.8 collective-permute-start.10
  45.0 1.4 collective-permute-done.10.other_ref
  46.4 1.3 copy-done.12
  47.7 5.4 %shard_map.114 = (f32[8,48,1152]{2,1,0:T(8,128)}, f32[2,24,4608]{2,1,0:T(8,128)S(1)}) custom-call(s32[4]{0:T(128)S(1)} %pad_add_fusion.here_ref, f32[48,4608]{1,0:T(8,128)S(1)} %get-tuple-element.21.orbital_ref, f32[48,2304]{1,0:T(8,128)S(1)} %concatenate.9.half_ref, f32[48,2304]{1,0:T(8,128)S(1)} %collective-permute-done.10.other_ref, ...), custom_call_target="tpu_custom_call" | custom-call | flops 2038431744 | bytes 4000000 | tf_op jit(solution)/shard_map/pallas_call | solution.py:449
  54.0 6.6 %all-to-all-start.2 = ((f32[8,48,1152]{2,1,0:T(8,128)}), f32[8,48,1152]{2,1,0:T(8,128)S(1)}, u32[]{:S(2)}, u32[]{:S(2)}) async-start(f32[8,48,1152]{2,1,0:T(8,128)} %get-tuple-element.31), calls=%async_computation.2 | async-start | bytes 3538944 | tf_op jit(solution)/shard_map/all_to_all | solution.py:508
  60.6 1.3 copy-done.11
  61.9 1.3 copy-done.13
  64.6 5.4 %shard_map.115 = (f32[8,48,1152]{2,1,0:T(8,128)}, f32[2,24,4608]{2,1,0:T(8,128)S(1)}) custom-call(s32[4]{0:T(128)S(1)} %pad_add_fusion.here_ref, f32[48,4608]{1,0:T(8,128)S(1)} %get-tuple-element.21.orbital_ref, f32[48,2304]{1,0:T(8,128)S(1)} %concatenate.9.half_ref, f32[48,2304]{1,0:T(8,128)S(1)} %collective-permute-done.10.other_ref, ...), custom_call_target="tpu_custom_call" | custom-call | flops 2038431744 | bytes 4000000 | tf_op jit(solution)/shard_map/pallas_call | solution.py:449
  71.0 12.3 %all-to-all-done.2.refs_0_ = f32[8,48,1152]{2,1,0:T(8,128)S(1)} async-done(((f32[8,48,1152]{2,1,0:T(8,128)}), f32[8,48,1152]{2,1,0:T(8,128)S(1)}, u32[]{:S(2)}, u32[]{:S(2)}) %all-to-all-start.2) | async-done | bytes 1769504 | tf_op jit(solution)/shard_map/all_to_all | solution.py:508
  83.3 5.2 %all-to-all-start = ((f32[8,48,1152]{2,1,0:T(8,128)}), f32[8,48,1152]{2,1,0:T(8,128)S(1)}, u32[]{:S(2)}, u32[]{:S(2)}) async-start(f32[8,48,1152]{2,1,0:T(8,128)} %get-tuple-element.28), calls=%async_computation | async-start | bytes 3538944 | tf_op jit(solution)/shard_map/all_to_all | solution.py:508
  90.2 5.7 %shard_map.117 = f32[8,48,1152]{2,1,0:T(8,128)S(1)} custom-call(s32[4]{0:T(128)S(1)} %pad_add_fusion.here_ref, f32[8,48,1152]{2,1,0:T(8,128)S(1)} %all-to-all-done.2.refs_0_, f32[192,1152]{1,0:T(8,128)S(1)} %fusion.1.refs_1_, bf16[384,576]{1,0:T(8,128)(2,1)S(1)} %copy-done.14), custom_call_target="tpu_custom_call" | custom-call | flops 2038431744 | bytes 4000000 | tf_op jit(solution)/shard_map/pallas_call | solution.py:471
  95.8 1.2 copy-done
  98.0 13.2 %all-to-all-done.refs_0_ = f32[8,48,1152]{2,1,0:T(8,128)S(1)} async-done(((f32[8,48,1152]{2,1,0:T(8,128)}), f32[8,48,1152]{2,1,0:T(8,128)S(1)}, u32[]{:S(2)}, u32[]{:S(2)}) %all-to-all-start) | async-done | bytes 1769504 | tf_op jit(solution)/shard_map/all_to_all | solution.py:508
  111.1 5.3 %all-to-all-start.3 = ((f32[8,48,1152]{2,1,0:T(8,128)}), f32[8,48,1152]{2,1,0:T(8,128)}, u32[]{:S(2)}, u32[]{:S(2)}) async-start(f32[8,48,1152]{2,1,0:T(8,128)} %copy-done), calls=%async_computation.3 | async-start | bytes 3538944 | tf_op jit(solution)/shard_map/all_to_all | solution.py:508
  116.5 6.9 %shard_map.116 = f32[8,48,1152]{2,1,0:T(8,128)} custom-call(s32[4]{0:T(128)S(1)} %pad_add_fusion.here_ref, f32[8,48,1152]{2,1,0:T(8,128)S(1)} %all-to-all-done.refs_0_, f32[192,1152]{1,0:T(8,128)S(1)} %copy-done.3, bf16[384,576]{1,0:T(8,128)(2,1)S(1)} %copy-done.15), custom_call_target="tpu_custom_call" | custom-call | flops 2038431744 | bytes 4000000 | tf_op jit(solution)/shard_map/pallas_call | solution.py:471
  123.4 15.8 %all-to-all-done.3.rest_0_ = f32[8,48,1152]{2,1,0:T(8,128)} async-done(((f32[8,48,1152]{2,1,0:T(8,128)}), f32[8,48,1152]{2,1,0:T(8,128)}, u32[]{:S(2)}, u32[]{:S(2)}) %all-to-all-start.3) | async-done | bytes 1769504 | tf_op jit(solution)/shard_map/all_to_all | solution.py:508
  139.2 5.2 %all-to-all-start.1 = ((f32[8,48,1152]{2,1,0:T(8,128)}), f32[8,48,1152]{2,1,0:T(8,128)}, u32[]{:S(2)}, u32[]{:S(2)}) async-start(f32[8,48,1152]{2,1,0:T(8,128)} %shard_map.116), calls=%async_computation.1 | async-start | bytes 3538944 | tf_op jit(solution)/shard_map/all_to_all | solution.py:508
  145.6 5.2 %shard_map.118 = (f32[48,4608]{1,0:T(8,128)S(1)}, f32[24,2304]{1,0:T(8,128)S(1)}, f32[24,2304]{1,0:T(8,128)S(1)}) custom-call(s32[4]{0:T(128)S(1)} %pad_add_fusion.here_ref, f32[48,4608]{1,0:T(8,128)S(1)} %copy-done.7, f32[2,24,4608]{2,1,0:T(8,128)S(1)} %copy-done.27, f32[12,384]{1,0:T(8,128)S(1)} %copy-done.21, f32[12,384]{1,0:T(8,128)S(1)} %copy-done.18, ...), custom_call_target="tpu_custom_call" | custom-call | flops 2038431744 | bytes 8000000 | tf_op jit(solution)/shard_map/pallas_call | solution.py:487
  153.7 1.7 collective-permute-start.14
  155.5 1.2 collective-permute-start.12
  156.9 1.5 collective-permute-done.14
  158.4 8.3 %collective-permute-done.12 = f32[24,576]{1,0:T(8,128)S(1)} collective-permute-done((f32[24,576]{1,0:T(8,128)S(1)}, f32[24,576]{1,0:T(8,128)S(1)}, u32[]{:S(2)}, u32[]{:S(2)}) %collective-permute-start.12) | collective-permute-done | bytes 55328 | tf_op jit(solution)/shard_map/ppermute | solution.py:48
  170.3 6.3 %shard_map.119 = (f32[12,4,4608]{2,1,0:T(4,128)}, f32[24,2304]{1,0:T(8,128)S(1)}, f32[24,2304]{1,0:T(8,128)S(1)}) custom-call(s32[4]{0:T(128)S(1)} %pad_add_fusion.here_ref, f32[48,4608]{1,0:T(8,128)S(1)} %copy-done.7, f32[2,24,4608]{2,1,0:T(8,128)S(1)} %copy-done.23, f32[12,384]{1,0:T(8,128)S(1)} %copy-done.21, f32[12,384]{1,0:T(8,128)S(1)} %copy-done.18, ...), custom_call_target="tpu_custom_call" | custom-call | flops 2038431744 | bytes 8000000 | tf_op jit(solution)/shard_map/pallas_call | solution.py:487
  176.6 2.4 %collective-permute-start.15 = (f32[24,2304]{1,0:T(8,128)S(1)}, f32[24,2304]{1,0:T(8,128)S(1)}, u32[]{:S(2)}, u32[]{:S(2)}) collective-permute-start(f32[24,2304]{1,0:T(8,128)S(1)} %get-tuple-element.39), channel_id=1, source_target_pairs={{0,8},{8,0},{1,9},{9,1},{2,10},{10,2},{3,11},{11,3},{4,12},{12,4},... | collective-permute-start | bytes 663560 | tf_op jit(solution)/shard_map/ppermute | solution.py:38
  180.3 1.5 collective-permute-start.18
  183.1 1.3 collective-permute-done.18
  184.4 2.0 collective-permute-done.16
  186.5 4.2 %collective-permute-start.20 = (f32[48,576]{1,0:T(8,128)S(1)}, f32[48,576]{1,0:T(8,128)S(1)}, u32[]{:S(2)}, u32[]{:S(2)}) collective-permute-start(f32[48,576]{1,0:T(8,128)S(1)} %pad_maximum_fusion), channel_id=1, source_target_pairs={{0,128},{32,160},{64,192},{96,224},{128,0},{160,32},{192,64},{224,... | collective-permute-start | bytes 331784 | tf_op jit(solution)/shard_map/ppermute | solution.py:53
  191.1 2.1 collective-permute-start.19
  193.1 1.2 collective-permute-done.20
  194.3 9.4 %collective-permute-done.21 = f32[48,576]{1,0:T(8,128)S(1)} collective-permute-done((f32[48,576]{1,0:T(8,128)S(1)}, f32[48,576]{1,0:T(8,128)S(1)}, u32[]{:S(2)}, u32[]{:S(2)}) %collective-permute-start.21) | collective-permute-done | bytes 110624 | tf_op jit(solution)/shard_map/ppermute | solution.py:53
  204.8 1.4 collective-permute-start.23
  206.5 2.6 %collective-permute-done.24 = f32[48,576]{1,0:T(8,128)S(1)} collective-permute-done((f32[48,576]{1,0:T(8,128)S(1)}, f32[48,576]{1,0:T(8,128)S(1)}, u32[]{:S(2)}, u32[]{:S(2)}) %collective-permute-start.24) | collective-permute-done | bytes 110624 | tf_op jit(solution)/shard_map/ppermute | solution.py:48
  209.1 2.7 %collective-permute-done.23 = f32[48,576]{1,0:T(8,128)S(1)} collective-permute-done((f32[48,576]{1,0:T(8,128)S(1)}, f32[48,576]{1,0:T(8,128)S(1)}, u32[]{:S(2)}, u32[]{:S(2)}) %collective-permute-start.23) | collective-permute-done | bytes 110624 | tf_op jit(solution)/shard_map/ppermute | solution.py:48
  212.2 1.3 collective-permute-start.25
  213.4 1.4 collective-permute-done.25.other_ref
  214.9 1.7 shard_map.120
  (102 shorter events, 26.9 us)
Async XLA Ops:
  0.7 1.2 copy-start.1
  4.3 56.4 %copy-start.6 = (f32[48,4608]{1,0:T(8,128)}, f32[48,4608]{1,0:T(8,128)S(1)}, u32[]{:S(2)}) copy-start(f32[48,4608]{1,0:T(8,128)S(1)} %get-tuple-element.21.orbital_ref) | copy-start | bytes 2654212
  4.3 4.7 %collective-permute-start = (f32[48,2304]{1,0:T(8,128)S(1)}, f32[48,2304]{1,0:T(8,128)S(1)}, u32[]{:S(2)}, u32[]{:S(2)}) collective-permute-start(f32[48,2304]{1,0:T(8,128)S(1)} %get-tuple-element.23), channel_id=1, source_target_pairs={{0,8},{8,0},{1,9},{9,1},{2,10},{10,2},{3,11},{11,3},{4,12},{12,4},... | collective-permute-start | bytes 1327112 | tf_op jit(solution)/shard_map/ppermute | solution.py:38
  9.2 5.5 %collective-permute-start.3 = (f32[48,576]{1,0:T(8,128)S(1)}, f32[48,576]{1,0:T(8,128)S(1)}, u32[]{:S(2)}, u32[]{:S(2)}) collective-permute-start(f32[48,576]{1,0:T(8,128)S(1)} %select_select_fusion.8), channel_id=1, source_target_pairs={{0,48},{16,32},{32,16},{48,0},{64,112},{80,96},{96,80},{112,64},{1... | collective-permute-start | bytes 331784 | tf_op jit(solution)/shard_map/ppermute | solution.py:48
  10.3 36.2 %copy-start.10 = (bf16[768,768]{1,0:T(8,128)(2,1)S(1)}, bf16[768,768]{1,0:T(8,128)(2,1)}, u32[]{:S(2)}) copy-start(bf16[768,768]{1,0:T(8,128)(2,1)} %constant.146.clone.low_source) | copy-start | bytes 3538948
  10.3 36.2 %copy-start.16 = (f32[12,384]{1,0:T(8,128)S(1)}, f32[12,384]{1,0:T(8,128)}, u32[]{:S(2)}) copy-start(f32[12,384]{1,0:T(8,128)} %constant.144.clone.sin_ref) | copy-start | bytes 55300
  10.3 36.1 %copy-start.19 = (f32[12,384]{1,0:T(8,128)S(1)}, f32[12,384]{1,0:T(8,128)}, u32[]{:S(2)}) copy-start(f32[12,384]{1,0:T(8,128)} %constant.143.clone.cos_ref) | copy-start | bytes 55300
  10.3 7.8 %collective-permute-start.1 = (f32[48,576]{1,0:T(8,128)S(1)}, f32[48,576]{1,0:T(8,128)S(1)}, u32[]{:S(2)}, u32[]{:S(2)}) collective-permute-start(f32[48,576]{1,0:T(8,128)S(1)} %get-tuple-element.48), channel_id=1, source_target_pairs={{0,16},{16,0},{32,48},{48,32},{64,80},{80,64},{96,112},{112,96},{1... | collective-permute-start | bytes 331784 | tf_op jit(solution)/shard_map/ppermute | solution.py:48
  10.6 7.4 %collective-permute-start.2 = (f32[48,576]{1,0:T(8,128)S(1)}, f32[48,576]{1,0:T(8,128)S(1)}, u32[]{:S(2)}, u32[]{:S(2)}) collective-permute-start(f32[48,576]{1,0:T(8,128)S(1)} %get-tuple-element.49), channel_id=1, source_target_pairs={{0,32},{16,48},{32,0},{48,16},{64,96},{80,112},{96,64},{112,80},{1... | collective-permute-start | bytes 331784 | tf_op jit(solution)/shard_map/ppermute | solution.py:48
  18.2 8.6 %collective-permute-start.6 = (f32[48,576]{1,0:T(8,128)S(1)}, f32[48,576]{1,0:T(8,128)S(1)}, u32[]{:S(2)}, u32[]{:S(2)}) collective-permute-start(f32[48,576]{1,0:T(8,128)S(1)} %add_add_fusion.2), channel_id=1, source_target_pairs={{0,192},{32,224},{64,0},{96,32},{128,64},{160,96},{192,128},{224,1... | collective-permute-start | bytes 331784 | tf_op jit(solution)/shard_map/ppermute | solution.py:53
  22.6 11.1 %collective-permute-start.5 = (f32[48,576]{1,0:T(8,128)S(1)}, f32[48,576]{1,0:T(8,128)S(1)}, u32[]{:S(2)}, u32[]{:S(2)}) collective-permute-start(f32[48,576]{1,0:T(8,128)S(1)} %add_add_fusion.2), channel_id=1, source_target_pairs={{0,128},{32,160},{64,192},{96,224},{128,0},{160,32},{192,64},{224,... | collective-permute-start | bytes 331784 | tf_op jit(solution)/shard_map/ppermute | solution.py:53
  23.6 10.1 %collective-permute-start.4 = (f32[48,576]{1,0:T(8,128)S(1)}, f32[48,576]{1,0:T(8,128)S(1)}, u32[]{:S(2)}, u32[]{:S(2)}) collective-permute-start(f32[48,576]{1,0:T(8,128)S(1)} %add_add_fusion.2), channel_id=1, source_target_pairs={{0,64},{32,96},{64,128},{96,160},{128,192},{160,224},{192,0},{224,... | collective-permute-start | bytes 331784 | tf_op jit(solution)/shard_map/ppermute | solution.py:53
  33.7 6.2 %collective-permute-start.9 = (f32[48,576]{1,0:T(8,128)S(1)}, f32[48,576]{1,0:T(8,128)S(1)}, u32[]{:S(2)}, u32[]{:S(2)}) collective-permute-start(f32[48,576]{1,0:T(8,128)S(1)} %add_add_fusion.1), channel_id=1, source_target_pairs={{0,48},{16,32},{32,16},{48,0},{64,112},{80,96},{96,80},{112,64},{1... | collective-permute-start | bytes 331784 | tf_op jit(solution)/shard_map/ppermute | solution.py:48
  37.6 5.0 %collective-permute-start.8 = (f32[48,576]{1,0:T(8,128)S(1)}, f32[48,576]{1,0:T(8,128)S(1)}, u32[]{:S(2)}, u32[]{:S(2)}) collective-permute-start(f32[48,576]{1,0:T(8,128)S(1)} %add_add_fusion.1), channel_id=1, source_target_pairs={{0,32},{16,48},{32,0},{48,16},{64,96},{80,112},{96,64},{112,80},{1... | collective-permute-start | bytes 331784 | tf_op jit(solution)/shard_map/ppermute | solution.py:48
  37.6 5.3 %collective-permute-start.7 = (f32[48,576]{1,0:T(8,128)S(1)}, f32[48,576]{1,0:T(8,128)S(1)}, u32[]{:S(2)}, u32[]{:S(2)}) collective-permute-start(f32[48,576]{1,0:T(8,128)S(1)} %add_add_fusion.1), channel_id=1, source_target_pairs={{0,16},{16,0},{32,48},{48,32},{64,80},{80,64},{96,112},{112,96},{1... | collective-permute-start | bytes 331784 | tf_op jit(solution)/shard_map/ppermute | solution.py:48
  43.2 3.2 %collective-permute-start.10 = (f32[48,2304]{1,0:T(8,128)S(1)}, f32[48,2304]{1,0:T(8,128)S(1)}, u32[]{:S(2)}, u32[]{:S(2)}) collective-permute-start(f32[48,2304]{1,0:T(8,128)S(1)} %concatenate.9.half_ref), channel_id=1, source_target_pairs={{0,8},{8,0},{1,9},{9,1},{2,10},{10,2},{3,11},{11,3},{4,12},{12,4},... | collective-permute-start | bytes 1327112 | tf_op jit(solution)/shard_map/ppermute | solution.py:38
  46.4 1.3 copy-start.12
  54.0 29.2 %all-to-all-start.2 = ((f32[8,48,1152]{2,1,0:T(8,128)}), f32[8,48,1152]{2,1,0:T(8,128)S(1)}, u32[]{:S(2)}, u32[]{:S(2)}) async-start(f32[8,48,1152]{2,1,0:T(8,128)} %get-tuple-element.31), calls=%async_computation.2 | async-start | bytes 3538944 | tf_op jit(solution)/shard_map/all_to_all | solution.py:508
  60.6 1.3 copy-start.11
  61.9 1.3 copy-start.13
  83.3 27.8 %all-to-all-start = ((f32[8,48,1152]{2,1,0:T(8,128)}), f32[8,48,1152]{2,1,0:T(8,128)S(1)}, u32[]{:S(2)}, u32[]{:S(2)}) async-start(f32[8,48,1152]{2,1,0:T(8,128)} %get-tuple-element.28), calls=%async_computation | async-start | bytes 3538944 | tf_op jit(solution)/shard_map/all_to_all | solution.py:508
  95.8 1.2 copy-start
  98.0 18.5 %copy-start.15 = (bf16[384,576]{1,0:T(8,128)(2,1)S(1)}, bf16[384,576]{1,0:T(8,128)(2,1)}, u32[]{:S(2)}) copy-start(bf16[384,576]{1,0:T(8,128)(2,1)} %constant.147.clone.refs_2_) | copy-start | bytes 1327108
  111.1 5.3 %copy-start.3 = (f32[192,1152]{1,0:T(8,128)S(1)}, f32[192,1152]{1,0:T(8,128)}, u32[]{:S(2)}) copy-start(f32[192,1152]{1,0:T(8,128)} %copy-done.2) | copy-start | bytes 2654212
  111.1 28.1 %all-to-all-start.3 = ((f32[8,48,1152]{2,1,0:T(8,128)}), f32[8,48,1152]{2,1,0:T(8,128)}, u32[]{:S(2)}, u32[]{:S(2)}) async-start(f32[8,48,1152]{2,1,0:T(8,128)} %copy-done), calls=%async_computation.3 | async-start | bytes 3538944 | tf_op jit(solution)/shard_map/all_to_all | solution.py:508
  123.3 21.1 %copy-start.7 = (f32[48,4608]{1,0:T(8,128)S(1)}, f32[48,4608]{1,0:T(8,128)}, u32[]{:S(2)}) copy-start(f32[48,4608]{1,0:T(8,128)} %copy-done.6) | copy-start | bytes 2654212
  123.3 21.1 %copy-start.8 = (bf16[768,768]{1,0:T(8,128)(2,1)S(1)}, bf16[768,768]{1,0:T(8,128)(2,1)}, u32[]{:S(2)}) copy-start(bf16[768,768]{1,0:T(8,128)(2,1)} %constant.149.clone.low_source) | copy-start | bytes 3538948
  123.3 21.1 %copy-start.9 = (bf16[768,768]{1,0:T(8,128)(2,1)S(1)}, bf16[768,768]{1,0:T(8,128)(2,1)}, u32[]{:S(2)}) copy-start(bf16[768,768]{1,0:T(8,128)(2,1)} %constant.148.clone.high_source) | copy-start | bytes 3538948
  123.3 21.1 %copy-start.18 = (f32[12,384]{1,0:T(8,128)S(1)}, f32[12,384]{1,0:T(8,128)}, u32[]{:S(2)}) copy-start(f32[12,384]{1,0:T(8,128)} %constant.144.clone.sin_ref) | copy-start | bytes 55300
  123.3 21.1 %copy-start.21 = (f32[12,384]{1,0:T(8,128)S(1)}, f32[12,384]{1,0:T(8,128)}, u32[]{:S(2)}) copy-start(f32[12,384]{1,0:T(8,128)} %constant.143.clone.cos_ref) | copy-start | bytes 55300
  139.2 28.7 %all-to-all-start.1 = ((f32[8,48,1152]{2,1,0:T(8,128)}), f32[8,48,1152]{2,1,0:T(8,128)}, u32[]{:S(2)}, u32[]{:S(2)}) async-start(f32[8,48,1152]{2,1,0:T(8,128)} %shard_map.116), calls=%async_computation.1 | async-start | bytes 3538944 | tf_op jit(solution)/shard_map/all_to_all | solution.py:508
  144.4 1.2 copy-start.27
  151.7 1.9 collective-permute-start.11
  153.7 4.7 %collective-permute-start.14 = (f32[24,576]{1,0:T(8,128)S(1)}, f32[24,576]{1,0:T(8,128)S(1)}, u32[]{:S(2)}, u32[]{:S(2)}) collective-permute-start(f32[24,576]{1,0:T(8,128)S(1)} %select_select_fusion.14), channel_id=1, source_target_pairs={{0,48},{16,32},{32,16},{48,0},{64,112},{80,96},{96,80},{112,64},{1... | collective-permute-start | bytes 165896 | tf_op jit(solution)/shard_map/ppermute | solution.py:48
  155.5 11.2 %collective-permute-start.12 = (f32[24,576]{1,0:T(8,128)S(1)}, f32[24,576]{1,0:T(8,128)S(1)}, u32[]{:S(2)}, u32[]{:S(2)}) collective-permute-start(f32[24,576]{1,0:T(8,128)S(1)} %get-tuple-element.52), channel_id=1, source_target_pairs={{0,16},{16,0},{32,48},{48,32},{64,80},{80,64},{96,112},{112,96},{1... | collective-permute-start | bytes 165896 | tf_op jit(solution)/shard_map/ppermute | solution.py:48
  156.8 10.0 %collective-permute-start.13 = (f32[24,576]{1,0:T(8,128)S(1)}, f32[24,576]{1,0:T(8,128)S(1)}, u32[]{:S(2)}, u32[]{:S(2)}) collective-permute-start(f32[24,576]{1,0:T(8,128)S(1)} %get-tuple-element.53), channel_id=1, source_target_pairs={{0,32},{16,48},{32,0},{48,16},{64,96},{80,112},{96,64},{112,80},{1... | collective-permute-start | bytes 165896 | tf_op jit(solution)/shard_map/ppermute | solution.py:48
  176.6 9.9 %copy-start.28 = (f32[24,576]{1,0:T(8,128)S(1)}, f32[24,576]{1,0:T(8,128)}, u32[]{:S(2)}) copy-start(f32[24,576]{1,0:T(8,128)} %add_add_fusion.4) | copy-start | bytes 165892
  176.6 3.5 %collective-permute-start.15 = (f32[24,2304]{1,0:T(8,128)S(1)}, f32[24,2304]{1,0:T(8,128)S(1)}, u32[]{:S(2)}, u32[]{:S(2)}) collective-permute-start(f32[24,2304]{1,0:T(8,128)S(1)} %get-tuple-element.39), channel_id=1, source_target_pairs={{0,8},{8,0},{1,9},{9,1},{2,10},{10,2},{3,11},{11,3},{4,12},{12,4},... | collective-permute-start | bytes 663560 | tf_op jit(solution)/shard_map/ppermute | solution.py:38
  180.3 4.1 %collective-permute-start.18 = (f32[24,576]{1,0:T(8,128)S(1)}, f32[24,576]{1,0:T(8,128)S(1)}, u32[]{:S(2)}, u32[]{:S(2)}) collective-permute-start(f32[24,576]{1,0:T(8,128)S(1)} %select_select_fusion.11), channel_id=1, source_target_pairs={{0,48},{16,32},{32,16},{48,0},{64,112},{80,96},{96,80},{112,64},{1... | collective-permute-start | bytes 165896 | tf_op jit(solution)/shard_map/ppermute | solution.py:48
  181.8 4.6 %collective-permute-start.16 = (f32[24,576]{1,0:T(8,128)S(1)}, f32[24,576]{1,0:T(8,128)S(1)}, u32[]{:S(2)}, u32[]{:S(2)}) collective-permute-start(f32[24,576]{1,0:T(8,128)S(1)} %get-tuple-element.50), channel_id=1, source_target_pairs={{0,16},{16,0},{32,48},{48,32},{64,80},{80,64},{96,112},{112,96},{1... | collective-permute-start | bytes 165896 | tf_op jit(solution)/shard_map/ppermute | solution.py:48
  183.0 3.4 %collective-permute-start.17 = (f32[24,576]{1,0:T(8,128)S(1)}, f32[24,576]{1,0:T(8,128)S(1)}, u32[]{:S(2)}, u32[]{:S(2)}) collective-permute-start(f32[24,576]{1,0:T(8,128)S(1)} %get-tuple-element.51), channel_id=1, source_target_pairs={{0,32},{16,48},{32,0},{48,16},{64,96},{80,112},{96,64},{112,80},{1... | collective-permute-start | bytes 165896 | tf_op jit(solution)/shard_map/ppermute | solution.py:48
  186.5 7.8 %collective-permute-start.20 = (f32[48,576]{1,0:T(8,128)S(1)}, f32[48,576]{1,0:T(8,128)S(1)}, u32[]{:S(2)}, u32[]{:S(2)}) collective-permute-start(f32[48,576]{1,0:T(8,128)S(1)} %pad_maximum_fusion), channel_id=1, source_target_pairs={{0,128},{32,160},{64,192},{96,224},{128,0},{160,32},{192,64},{224,... | collective-permute-start | bytes 331784 | tf_op jit(solution)/shard_map/ppermute | solution.py:53
  190.7 13.0 %collective-permute-start.21 = (f32[48,576]{1,0:T(8,128)S(1)}, f32[48,576]{1,0:T(8,128)S(1)}, u32[]{:S(2)}, u32[]{:S(2)}) collective-permute-start(f32[48,576]{1,0:T(8,128)S(1)} %pad_maximum_fusion), channel_id=1, source_target_pairs={{0,192},{32,224},{64,0},{96,32},{128,64},{160,96},{192,128},{224,1... | collective-permute-start | bytes 331784 | tf_op jit(solution)/shard_map/ppermute | solution.py:53
  191.1 12.7 %collective-permute-start.19 = (f32[48,576]{1,0:T(8,128)S(1)}, f32[48,576]{1,0:T(8,128)S(1)}, u32[]{:S(2)}, u32[]{:S(2)}) collective-permute-start(f32[48,576]{1,0:T(8,128)S(1)} %pad_maximum_fusion), channel_id=1, source_target_pairs={{0,64},{32,96},{64,128},{96,160},{128,192},{160,224},{192,0},{224,... | collective-permute-start | bytes 331784 | tf_op jit(solution)/shard_map/ppermute | solution.py:53
  203.7 5.3 %collective-permute-start.24 = (f32[48,576]{1,0:T(8,128)S(1)}, f32[48,576]{1,0:T(8,128)S(1)}, u32[]{:S(2)}, u32[]{:S(2)}) collective-permute-start(f32[48,576]{1,0:T(8,128)S(1)} %add_add_fusion), channel_id=1, source_target_pairs={{0,48},{16,32},{32,16},{48,0},{64,112},{80,96},{96,80},{112,64},{1... | collective-permute-start | bytes 331784 | tf_op jit(solution)/shard_map/ppermute | solution.py:48
  204.8 6.9 %collective-permute-start.23 = (f32[48,576]{1,0:T(8,128)S(1)}, f32[48,576]{1,0:T(8,128)S(1)}, u32[]{:S(2)}, u32[]{:S(2)}) collective-permute-start(f32[48,576]{1,0:T(8,128)S(1)} %add_add_fusion), channel_id=1, source_target_pairs={{0,32},{16,48},{32,0},{48,16},{64,96},{80,112},{96,64},{112,80},{1... | collective-permute-start | bytes 331784 | tf_op jit(solution)/shard_map/ppermute | solution.py:48
  206.2 5.7 %collective-permute-start.22 = (f32[48,576]{1,0:T(8,128)S(1)}, f32[48,576]{1,0:T(8,128)S(1)}, u32[]{:S(2)}, u32[]{:S(2)}) collective-permute-start(f32[48,576]{1,0:T(8,128)S(1)} %add_add_fusion), channel_id=1, source_target_pairs={{0,16},{16,0},{32,48},{48,32},{64,80},{80,64},{96,112},{112,96},{1... | collective-permute-start | bytes 331784 | tf_op jit(solution)/shard_map/ppermute | solution.py:48
  212.2 2.7 %collective-permute-start.25 = (f32[48,2304]{1,0:T(8,128)S(1)}, f32[48,2304]{1,0:T(8,128)S(1)}, u32[]{:S(2)}, u32[]{:S(2)}) collective-permute-start(f32[48,2304]{1,0:T(8,128)S(1)} %concatenate.11.own_ref), channel_id=1, source_target_pairs={{0,8},{8,0},{1,9},{9,1},{2,10},{10,2},{3,11},{11,3},{4,12},{12,4},... | collective-permute-start | bytes 1327112 | tf_op jit(solution)/shard_map/ppermute | solution.py:38
  (11 other events, 9.9 us)

commit v3 on v2

--- a/solution.py
+++ b/solution.py
@@ -76,8 +76,8 @@
 
 
 def join_far(part):
-    arrived = [along(part, distance) for distance in (2, 4, 6)]
-    return part + arrived[0] + arrived[1] + arrived[2]
+    above, below, across = [along(part, distance) for distance in (6, 2, 4)]
+    return (part + across) + (below + above)
 
 
 def spread_near(part):

time: 217 us -> 216 us (level)
  waiting for transfers between devices: 96.1 us -> 93.2 us
    ppermute x15, starting transfers between devices: 15.7 us -> 18.1 us  [near(): return lax.ppermute(x, ('z', 'xl'), pairs)]
  transfers between devices with their start and end apart: 30 -> 30, of which waited for: 25 -> 28; matrix products, arithmetic and copies ran while one was open for 1% -> 1% of each run, Pallas kernels for 11% -> 11%
where the time goes in v3:
time: 216 us
  waiting for transfers between devices  93.2 us (43%)
  starting transfers between devices  63.8 us (30%)
  Pallas kernels  37.5 us (17%)
  local copies, waits for them, and re-layouts  17.6 us (8%)
  other arithmetic  2.64 us (1%)
    all_to_all x4, waiting for transfers between devices, exchange(): lax.all_to_all(pieces[0], ('xh', 'y'), split_axis=0, concat_axis=0, tiled...  41.9 us
    ppermute x15, waiting for transfers between devices, near(): return lax.ppermute(x, ('z', 'xl'), pairs)  28.5 us
    all_to_all x4, starting transfers between devices, exchange(): lax.all_to_all(pieces[0], ('xh', 'y'), split_axis=0, concat_axis=0, tiled...  22 us
    ppermute x15, starting transfers between devices, near(): return lax.ppermute(x, ('z', 'xl'), pairs)  18.1 us
    unnamed x58, local copies, waits for them, and re-layouts  17.2 us
    ppermute x6, waiting for transfers between devices, along(): lax.ppermute(x, 'z', [(i, (i + distance) % size) for i in range(size)])  16.3 us
    ppermute x6, starting transfers between devices, along(): lax.ppermute(x, 'z', [(i, (i + distance) % size) for i in range(size)])  12.9 us
    pallas_call x2, Pallas kernels, screened(): pl.pallas_call(functools.partial(middle_kernel, whole), out_shape=shapes,...  12.5 us
  transfers between devices with their start and end apart: 30, of which 28 were waited for; matrix products, arithmetic and copies ran while one was open for 1% of the time, Pallas kernels for 11%

profile of v3, /device:TPU:1, one launch (start us, length us, event | category | flops | bytes accessed | tf_op | source)
XLA Modules:
  0.0 215.6 jit_solution(5028236558904598339)
XLA Ops:
  4.3 3.3 %collective-permute-start = (f32[48,2304]{1,0:T(8,128)S(1)}, f32[48,2304]{1,0:T(8,128)S(1)}, u32[]{:S(2)}, u32[]{:S(2)}) collective-permute-start(f32[48,2304]{1,0:T(8,128)S(1)} %get-tuple-element.23), channel_id=1, source_target_pairs={{0,8},{8,0},{1,9},{9,1},{2,10},{10,2},{3,11},{11,3},{4,12},{12,4},... | collective-permute-start | bytes 1327112 | tf_op jit(solution)/shard_map/ppermute | solution.py:38
  7.6 1.4 collective-permute-done
  10.6 1.6 collective-permute-start.2
  12.2 2.5 %collective-permute-done.3 = f32[48,576]{1,0:T(8,128)S(1)} collective-permute-done((f32[48,576]{1,0:T(8,128)S(1)}, f32[48,576]{1,0:T(8,128)S(1)}, u32[]{:S(2)}, u32[]{:S(2)}) %collective-permute-start.3) | collective-permute-done | bytes 110624 | tf_op jit(solution)/shard_map/ppermute | solution.py:48
  14.7 3.3 %collective-permute-done.1 = f32[48,576]{1,0:T(8,128)S(1)} collective-permute-done((f32[48,576]{1,0:T(8,128)S(1)}, f32[48,576]{1,0:T(8,128)S(1)}, u32[]{:S(2)}, u32[]{:S(2)}) %collective-permute-start.1) | collective-permute-done | bytes 110624 | tf_op jit(solution)/shard_map/ppermute | solution.py:48
  18.2 4.4 %collective-permute-start.6 = (f32[48,576]{1,0:T(8,128)S(1)}, f32[48,576]{1,0:T(8,128)S(1)}, u32[]{:S(2)}, u32[]{:S(2)}) collective-permute-start(f32[48,576]{1,0:T(8,128)S(1)} %add_add_fusion.2), channel_id=1, source_target_pairs={{0,192},{32,224},{64,0},{96,32},{128,64},{160,96},{192,128},{224,1... | collective-permute-start | bytes 331784 | tf_op jit(solution)/shard_map/ppermute | solution.py:53
  22.6 3.3 %collective-permute-start.4 = (f32[48,576]{1,0:T(8,128)S(1)}, f32[48,576]{1,0:T(8,128)S(1)}, u32[]{:S(2)}, u32[]{:S(2)}) collective-permute-start(f32[48,576]{1,0:T(8,128)S(1)} %add_add_fusion.2), channel_id=1, source_target_pairs={{0,128},{32,160},{64,192},{96,224},{128,0},{160,32},{192,64},{224,... | collective-permute-start | bytes 331784 | tf_op jit(solution)/shard_map/ppermute | solution.py:53
  26.9 3.0 %collective-permute-done.5 = f32[48,576]{1,0:T(8,128)S(1)} collective-permute-done((f32[48,576]{1,0:T(8,128)S(1)}, f32[48,576]{1,0:T(8,128)S(1)}, u32[]{:S(2)}, u32[]{:S(2)}) %collective-permute-start.5) | collective-permute-done | bytes 110624 | tf_op jit(solution)/shard_map/ppermute | solution.py:53
  29.9 3.6 %collective-permute-done.4 = f32[48,576]{1,0:T(8,128)S(1)} collective-permute-done((f32[48,576]{1,0:T(8,128)S(1)}, f32[48,576]{1,0:T(8,128)S(1)}, u32[]{:S(2)}, u32[]{:S(2)}) %collective-permute-start.4) | collective-permute-done | bytes 110624 | tf_op jit(solution)/shard_map/ppermute | solution.py:53
  33.6 4.1 %collective-permute-start.9 = (f32[48,576]{1,0:T(8,128)S(1)}, f32[48,576]{1,0:T(8,128)S(1)}, u32[]{:S(2)}, u32[]{:S(2)}) collective-permute-start(f32[48,576]{1,0:T(8,128)S(1)} %add_add_fusion.1), channel_id=1, source_target_pairs={{0,48},{16,32},{32,16},{48,0},{64,112},{80,96},{96,80},{112,64},{1... | collective-permute-start | bytes 331784 | tf_op jit(solution)/shard_map/ppermute | solution.py:48
  38.0 1.9 collective-permute-done.9
  39.9 2.8 %collective-permute-done.8 = f32[48,576]{1,0:T(8,128)S(1)} collective-permute-done((f32[48,576]{1,0:T(8,128)S(1)}, f32[48,576]{1,0:T(8,128)S(1)}, u32[]{:S(2)}, u32[]{:S(2)}) %collective-permute-start.8) | collective-permute-done | bytes 110624 | tf_op jit(solution)/shard_map/ppermute | solution.py:48
  43.2 2.5 %collective-permute-start.10 = (f32[48,2304]{1,0:T(8,128)S(1)}, f32[48,2304]{1,0:T(8,128)S(1)}, u32[]{:S(2)}, u32[]{:S(2)}) collective-permute-start(f32[48,2304]{1,0:T(8,128)S(1)} %concatenate.9.half_ref), channel_id=1, source_target_pairs={{0,8},{8,0},{1,9},{9,1},{2,10},{10,2},{3,11},{11,3},{4,12},{12,4},... | collective-permute-start | bytes 1327112 | tf_op jit(solution)/shard_map/ppermute | solution.py:38
  45.6 1.4 collective-permute-done.10.other_ref
  47.1 1.3 copy-done.12
  48.3 5.4 %shard_map.114 = (f32[8,48,1152]{2,1,0:T(8,128)}, f32[2,24,4608]{2,1,0:T(8,128)S(1)}) custom-call(s32[4]{0:T(128)S(1)} %pad_add_fusion.here_ref, f32[48,4608]{1,0:T(8,128)S(1)} %get-tuple-element.21.orbital_ref, f32[48,2304]{1,0:T(8,128)S(1)} %concatenate.9.half_ref, f32[48,2304]{1,0:T(8,128)S(1)} %collective-permute-done.10.other_ref, ...), custom_call_target="tpu_custom_call" | custom-call | flops 2038431744 | bytes 4000000 | tf_op jit(solution)/shard_map/pallas_call | solution.py:449
  54.7 6.3 %all-to-all-start.2 = ((f32[8,48,1152]{2,1,0:T(8,128)}), f32[8,48,1152]{2,1,0:T(8,128)S(1)}, u32[]{:S(2)}, u32[]{:S(2)}) async-start(f32[8,48,1152]{2,1,0:T(8,128)} %get-tuple-element.31), calls=%async_computation.2 | async-start | bytes 3538944 | tf_op jit(solution)/shard_map/all_to_all | solution.py:508
  61.0 1.3 copy-done.11
  62.3 1.3 copy-done.13
  65.0 5.4 %shard_map.115 = (f32[8,48,1152]{2,1,0:T(8,128)}, f32[2,24,4608]{2,1,0:T(8,128)S(1)}) custom-call(s32[4]{0:T(128)S(1)} %pad_add_fusion.here_ref, f32[48,4608]{1,0:T(8,128)S(1)} %get-tuple-element.21.orbital_ref, f32[48,2304]{1,0:T(8,128)S(1)} %concatenate.9.half_ref, f32[48,2304]{1,0:T(8,128)S(1)} %collective-permute-done.10.other_ref, ...), custom_call_target="tpu_custom_call" | custom-call | flops 2038431744 | bytes 4000000 | tf_op jit(solution)/shard_map/pallas_call | solution.py:449
  71.3 12.3 %all-to-all-done.2.refs_0_ = f32[8,48,1152]{2,1,0:T(8,128)S(1)} async-done(((f32[8,48,1152]{2,1,0:T(8,128)}), f32[8,48,1152]{2,1,0:T(8,128)S(1)}, u32[]{:S(2)}, u32[]{:S(2)}) %all-to-all-start.2) | async-done | bytes 1769504 | tf_op jit(solution)/shard_map/all_to_all | solution.py:508
  83.7 5.2 %all-to-all-start = ((f32[8,48,1152]{2,1,0:T(8,128)}), f32[8,48,1152]{2,1,0:T(8,128)S(1)}, u32[]{:S(2)}, u32[]{:S(2)}) async-start(f32[8,48,1152]{2,1,0:T(8,128)} %get-tuple-element.28), calls=%async_computation | async-start | bytes 3538944 | tf_op jit(solution)/shard_map/all_to_all | solution.py:508
  90.5 5.7 %shard_map.117 = f32[8,48,1152]{2,1,0:T(8,128)S(1)} custom-call(s32[4]{0:T(128)S(1)} %pad_add_fusion.here_ref, f32[8,48,1152]{2,1,0:T(8,128)S(1)} %all-to-all-done.2.refs_0_, f32[192,1152]{1,0:T(8,128)S(1)} %fusion.1.refs_1_, bf16[384,576]{1,0:T(8,128)(2,1)S(1)} %copy-done.14), custom_call_target="tpu_custom_call" | custom-call | flops 2038431744 | bytes 4000000 | tf_op jit(solution)/shard_map/pallas_call | solution.py:471
  98.3 13.1 %all-to-all-done.refs_0_ = f32[8,48,1152]{2,1,0:T(8,128)S(1)} async-done(((f32[8,48,1152]{2,1,0:T(8,128)}), f32[8,48,1152]{2,1,0:T(8,128)S(1)}, u32[]{:S(2)}, u32[]{:S(2)}) %all-to-all-start) | async-done | bytes 1769504 | tf_op jit(solution)/shard_map/all_to_all | solution.py:508
  111.5 5.3 %all-to-all-start.3 = ((f32[8,48,1152]{2,1,0:T(8,128)}), f32[8,48,1152]{2,1,0:T(8,128)}, u32[]{:S(2)}, u32[]{:S(2)}) async-start(f32[8,48,1152]{2,1,0:T(8,128)} %copy-done), calls=%async_computation.3 | async-start | bytes 3538944 | tf_op jit(solution)/shard_map/all_to_all | solution.py:508
  116.8 6.9 %shard_map.116 = f32[8,48,1152]{2,1,0:T(8,128)} custom-call(s32[4]{0:T(128)S(1)} %pad_add_fusion.here_ref, f32[8,48,1152]{2,1,0:T(8,128)S(1)} %all-to-all-done.refs_0_, f32[192,1152]{1,0:T(8,128)S(1)} %copy-done.3, bf16[384,576]{1,0:T(8,128)(2,1)S(1)} %copy-done.15), custom_call_target="tpu_custom_call" | custom-call | flops 2038431744 | bytes 4000000 | tf_op jit(solution)/shard_map/pallas_call | solution.py:471
  123.7 15.8 %all-to-all-done.3.rest_0_ = f32[8,48,1152]{2,1,0:T(8,128)} async-done(((f32[8,48,1152]{2,1,0:T(8,128)}), f32[8,48,1152]{2,1,0:T(8,128)}, u32[]{:S(2)}, u32[]{:S(2)}) %all-to-all-start.3) | async-done | bytes 1769504 | tf_op jit(solution)/shard_map/all_to_all | solution.py:508
  139.6 5.2 %all-to-all-start.1 = ((f32[8,48,1152]{2,1,0:T(8,128)}), f32[8,48,1152]{2,1,0:T(8,128)}, u32[]{:S(2)}, u32[]{:S(2)}) async-start(f32[8,48,1152]{2,1,0:T(8,128)} %shard_map.116), calls=%async_computation.1 | async-start | bytes 3538944 | tf_op jit(solution)/shard_map/all_to_all | solution.py:508
  146.0 5.2 %shard_map.118 = (f32[48,4608]{1,0:T(8,128)S(1)}, f32[24,2304]{1,0:T(8,128)S(1)}, f32[24,2304]{1,0:T(8,128)S(1)}) custom-call(s32[4]{0:T(128)S(1)} %pad_add_fusion.here_ref, f32[48,4608]{1,0:T(8,128)S(1)} %copy-done.7, f32[2,24,4608]{2,1,0:T(8,128)S(1)} %copy-done.27, f32[12,384]{1,0:T(8,128)S(1)} %copy-done.21, f32[12,384]{1,0:T(8,128)S(1)} %copy-done.18, ...), custom_call_target="tpu_custom_call" | custom-call | flops 2038431744 | bytes 8000000 | tf_op jit(solution)/shard_map/pallas_call | solution.py:487
  154.1 1.7 collective-permute-start.14
  155.9 1.6 collective-permute-start.12
  158.8 8.2 %collective-permute-done.12 = f32[24,576]{1,0:T(8,128)S(1)} collective-permute-done((f32[24,576]{1,0:T(8,128)S(1)}, f32[24,576]{1,0:T(8,128)S(1)}, u32[]{:S(2)}, u32[]{:S(2)}) %collective-permute-start.12) | collective-permute-done | bytes 55328 | tf_op jit(solution)/shard_map/ppermute | solution.py:48
  170.7 6.3 %shard_map.119 = (f32[12,4,4608]{2,1,0:T(4,128)}, f32[24,2304]{1,0:T(8,128)S(1)}, f32[24,2304]{1,0:T(8,128)S(1)}) custom-call(s32[4]{0:T(128)S(1)} %pad_add_fusion.here_ref, f32[48,4608]{1,0:T(8,128)S(1)} %copy-done.7, f32[2,24,4608]{2,1,0:T(8,128)S(1)} %copy-done.23, f32[12,384]{1,0:T(8,128)S(1)} %copy-done.21, f32[12,384]{1,0:T(8,128)S(1)} %copy-done.18, ...), custom_call_target="tpu_custom_call" | custom-call | flops 2038431744 | bytes 8000000 | tf_op jit(solution)/shard_map/pallas_call | solution.py:487
  176.9 2.4 %collective-permute-start.15 = (f32[24,2304]{1,0:T(8,128)S(1)}, f32[24,2304]{1,0:T(8,128)S(1)}, u32[]{:S(2)}, u32[]{:S(2)}) collective-permute-start(f32[24,2304]{1,0:T(8,128)S(1)} %get-tuple-element.39), channel_id=1, source_target_pairs={{0,8},{8,0},{1,9},{9,1},{2,10},{10,2},{3,11},{11,3},{4,12},{12,4},... | collective-permute-start | bytes 663560 | tf_op jit(solution)/shard_map/ppermute | solution.py:38
  180.7 1.5 collective-permute-start.18
  182.2 1.5 collective-permute-start.16
  184.8 2.0 collective-permute-done.16
  187.2 1.9 collective-permute-start.20
  189.0 1.8 collective-permute-start.21
  190.8 1.6 collective-permute-start.19
  192.4 1.3 collective-permute-done.20
  193.9 7.1 %collective-permute-done.19 = f32[48,576]{1,0:T(8,128)S(1)} collective-permute-done((f32[48,576]{1,0:T(8,128)S(1)}, f32[48,576]{1,0:T(8,128)S(1)}, u32[]{:S(2)}, u32[]{:S(2)}) %collective-permute-start.19) | collective-permute-done | bytes 110624 | tf_op jit(solution)/shard_map/ppermute | solution.py:53
  201.0 4.1 %collective-permute-start.24 = (f32[48,576]{1,0:T(8,128)S(1)}, f32[48,576]{1,0:T(8,128)S(1)}, u32[]{:S(2)}, u32[]{:S(2)}) collective-permute-start(f32[48,576]{1,0:T(8,128)S(1)} %add_add_fusion), channel_id=1, source_target_pairs={{0,48},{16,32},{32,16},{48,0},{64,112},{80,96},{96,80},{112,64},{1... | collective-permute-start | bytes 331784 | tf_op jit(solution)/shard_map/ppermute | solution.py:48
  205.6 1.9 collective-permute-done.24
  207.4 2.4 %collective-permute-done.23 = f32[48,576]{1,0:T(8,128)S(1)} collective-permute-done((f32[48,576]{1,0:T(8,128)S(1)}, f32[48,576]{1,0:T(8,128)S(1)}, u32[]{:S(2)}, u32[]{:S(2)}) %collective-permute-start.23) | collective-permute-done | bytes 110624 | tf_op jit(solution)/shard_map/ppermute | solution.py:48
  210.7 1.8 collective-permute-start.25
  212.5 1.4 collective-permute-done.25.other_ref
  214.0 1.7 shard_map.120
  (102 shorter events, 27.8 us)
Async XLA Ops:
  0.7 1.2 copy-start.1
  4.3 56.7 %copy-start.6 = (f32[48,4608]{1,0:T(8,128)}, f32[48,4608]{1,0:T(8,128)S(1)}, u32[]{:S(2)}) copy-start(f32[48,4608]{1,0:T(8,128)S(1)} %get-tuple-element.21.orbital_ref) | copy-start | bytes 2654212
  4.3 4.7 %collective-permute-start = (f32[48,2304]{1,0:T(8,128)S(1)}, f32[48,2304]{1,0:T(8,128)S(1)}, u32[]{:S(2)}, u32[]{:S(2)}) collective-permute-start(f32[48,2304]{1,0:T(8,128)S(1)} %get-tuple-element.23), channel_id=1, source_target_pairs={{0,8},{8,0},{1,9},{9,1},{2,10},{10,2},{3,11},{11,3},{4,12},{12,4},... | collective-permute-start | bytes 1327112 | tf_op jit(solution)/shard_map/ppermute | solution.py:38
  9.2 5.5 %collective-permute-start.3 = (f32[48,576]{1,0:T(8,128)S(1)}, f32[48,576]{1,0:T(8,128)S(1)}, u32[]{:S(2)}, u32[]{:S(2)}) collective-permute-start(f32[48,576]{1,0:T(8,128)S(1)} %select_select_fusion.8), channel_id=1, source_target_pairs={{0,48},{16,32},{32,16},{48,0},{64,112},{80,96},{96,80},{112,64},{1... | collective-permute-start | bytes 331784 | tf_op jit(solution)/shard_map/ppermute | solution.py:48
  10.3 36.8 %copy-start.10 = (bf16[768,768]{1,0:T(8,128)(2,1)S(1)}, bf16[768,768]{1,0:T(8,128)(2,1)}, u32[]{:S(2)}) copy-start(bf16[768,768]{1,0:T(8,128)(2,1)} %constant.146.clone.low_source) | copy-start | bytes 3538948
  10.3 36.8 %copy-start.16 = (f32[12,384]{1,0:T(8,128)S(1)}, f32[12,384]{1,0:T(8,128)}, u32[]{:S(2)}) copy-start(f32[12,384]{1,0:T(8,128)} %constant.144.clone.sin_ref) | copy-start | bytes 55300
  10.3 36.8 %copy-start.19 = (f32[12,384]{1,0:T(8,128)S(1)}, f32[12,384]{1,0:T(8,128)}, u32[]{:S(2)}) copy-start(f32[12,384]{1,0:T(8,128)} %constant.143.clone.cos_ref) | copy-start | bytes 55300
  10.3 7.8 %collective-permute-start.1 = (f32[48,576]{1,0:T(8,128)S(1)}, f32[48,576]{1,0:T(8,128)S(1)}, u32[]{:S(2)}, u32[]{:S(2)}) collective-permute-start(f32[48,576]{1,0:T(8,128)S(1)} %get-tuple-element.48), channel_id=1, source_target_pairs={{0,16},{16,0},{32,48},{48,32},{64,80},{80,64},{96,112},{112,96},{1... | collective-permute-start | bytes 331784 | tf_op jit(solution)/shard_map/ppermute | solution.py:48
  10.6 7.4 %collective-permute-start.2 = (f32[48,576]{1,0:T(8,128)S(1)}, f32[48,576]{1,0:T(8,128)S(1)}, u32[]{:S(2)}, u32[]{:S(2)}) collective-permute-start(f32[48,576]{1,0:T(8,128)S(1)} %get-tuple-element.49), channel_id=1, source_target_pairs={{0,32},{16,48},{32,0},{48,16},{64,96},{80,112},{96,64},{112,80},{1... | collective-permute-start | bytes 331784 | tf_op jit(solution)/shard_map/ppermute | solution.py:48
  18.2 8.6 %collective-permute-start.6 = (f32[48,576]{1,0:T(8,128)S(1)}, f32[48,576]{1,0:T(8,128)S(1)}, u32[]{:S(2)}, u32[]{:S(2)}) collective-permute-start(f32[48,576]{1,0:T(8,128)S(1)} %add_add_fusion.2), channel_id=1, source_target_pairs={{0,192},{32,224},{64,0},{96,32},{128,64},{160,96},{192,128},{224,1... | collective-permute-start | bytes 331784 | tf_op jit(solution)/shard_map/ppermute | solution.py:53
  22.6 7.3 %collective-permute-start.5 = (f32[48,576]{1,0:T(8,128)S(1)}, f32[48,576]{1,0:T(8,128)S(1)}, u32[]{:S(2)}, u32[]{:S(2)}) collective-permute-start(f32[48,576]{1,0:T(8,128)S(1)} %add_add_fusion.2), channel_id=1, source_target_pairs={{0,64},{32,96},{64,128},{96,160},{128,192},{160,224},{192,0},{224,... | collective-permute-start | bytes 331784 | tf_op jit(solution)/shard_map/ppermute | solution.py:53
  22.6 11.0 %collective-permute-start.4 = (f32[48,576]{1,0:T(8,128)S(1)}, f32[48,576]{1,0:T(8,128)S(1)}, u32[]{:S(2)}, u32[]{:S(2)}) collective-permute-start(f32[48,576]{1,0:T(8,128)S(1)} %add_add_fusion.2), channel_id=1, source_target_pairs={{0,128},{32,160},{64,192},{96,224},{128,0},{160,32},{192,64},{224,... | collective-permute-start | bytes 331784 | tf_op jit(solution)/shard_map/ppermute | solution.py:53
  33.6 6.3 %collective-permute-start.9 = (f32[48,576]{1,0:T(8,128)S(1)}, f32[48,576]{1,0:T(8,128)S(1)}, u32[]{:S(2)}, u32[]{:S(2)}) collective-permute-start(f32[48,576]{1,0:T(8,128)S(1)} %add_add_fusion.1), channel_id=1, source_target_pairs={{0,48},{16,32},{32,16},{48,0},{64,112},{80,96},{96,80},{112,64},{1... | collective-permute-start | bytes 331784 | tf_op jit(solution)/shard_map/ppermute | solution.py:48
  37.6 5.1 %collective-permute-start.8 = (f32[48,576]{1,0:T(8,128)S(1)}, f32[48,576]{1,0:T(8,128)S(1)}, u32[]{:S(2)}, u32[]{:S(2)}) collective-permute-start(f32[48,576]{1,0:T(8,128)S(1)} %add_add_fusion.1), channel_id=1, source_target_pairs={{0,32},{16,48},{32,0},{48,16},{64,96},{80,112},{96,64},{112,80},{1... | collective-permute-start | bytes 331784 | tf_op jit(solution)/shard_map/ppermute | solution.py:48
  37.7 5.3 %collective-permute-start.7 = (f32[48,576]{1,0:T(8,128)S(1)}, f32[48,576]{1,0:T(8,128)S(1)}, u32[]{:S(2)}, u32[]{:S(2)}) collective-permute-start(f32[48,576]{1,0:T(8,128)S(1)} %add_add_fusion.1), channel_id=1, source_target_pairs={{0,16},{16,0},{32,48},{48,32},{64,80},{80,64},{96,112},{112,96},{1... | collective-permute-start | bytes 331784 | tf_op jit(solution)/shard_map/ppermute | solution.py:48
  43.2 3.9 %collective-permute-start.10 = (f32[48,2304]{1,0:T(8,128)S(1)}, f32[48,2304]{1,0:T(8,128)S(1)}, u32[]{:S(2)}, u32[]{:S(2)}) collective-permute-start(f32[48,2304]{1,0:T(8,128)S(1)} %concatenate.9.half_ref), channel_id=1, source_target_pairs={{0,8},{8,0},{1,9},{9,1},{2,10},{10,2},{3,11},{11,3},{4,12},{12,4},... | collective-permute-start | bytes 1327112 | tf_op jit(solution)/shard_map/ppermute | solution.py:38
  47.0 1.3 copy-start.12
  54.7 29.0 %all-to-all-start.2 = ((f32[8,48,1152]{2,1,0:T(8,128)}), f32[8,48,1152]{2,1,0:T(8,128)S(1)}, u32[]{:S(2)}, u32[]{:S(2)}) async-start(f32[8,48,1152]{2,1,0:T(8,128)} %get-tuple-element.31), calls=%async_computation.2 | async-start | bytes 3538944 | tf_op jit(solution)/shard_map/all_to_all | solution.py:508
  61.0 1.3 copy-start.11
  62.3 1.3 copy-start.13
  83.7 27.8 %all-to-all-start = ((f32[8,48,1152]{2,1,0:T(8,128)}), f32[8,48,1152]{2,1,0:T(8,128)S(1)}, u32[]{:S(2)}, u32[]{:S(2)}) async-start(f32[8,48,1152]{2,1,0:T(8,128)} %get-tuple-element.28), calls=%async_computation | async-start | bytes 3538944 | tf_op jit(solution)/shard_map/all_to_all | solution.py:508
  96.2 1.2 copy-start
  98.3 18.5 %copy-start.15 = (bf16[384,576]{1,0:T(8,128)(2,1)S(1)}, bf16[384,576]{1,0:T(8,128)(2,1)}, u32[]{:S(2)}) copy-start(bf16[384,576]{1,0:T(8,128)(2,1)} %constant.147.clone.refs_2_) | copy-start | bytes 1327108
  111.5 5.3 %copy-start.3 = (f32[192,1152]{1,0:T(8,128)S(1)}, f32[192,1152]{1,0:T(8,128)}, u32[]{:S(2)}) copy-start(f32[192,1152]{1,0:T(8,128)} %copy-done.2) | copy-start | bytes 2654212
  111.5 28.1 %all-to-all-start.3 = ((f32[8,48,1152]{2,1,0:T(8,128)}), f32[8,48,1152]{2,1,0:T(8,128)}, u32[]{:S(2)}, u32[]{:S(2)}) async-start(f32[8,48,1152]{2,1,0:T(8,128)} %copy-done), calls=%async_computation.3 | async-start | bytes 3538944 | tf_op jit(solution)/shard_map/all_to_all | solution.py:508
  123.7 21.1 %copy-start.7 = (f32[48,4608]{1,0:T(8,128)S(1)}, f32[48,4608]{1,0:T(8,128)}, u32[]{:S(2)}) copy-start(f32[48,4608]{1,0:T(8,128)} %copy-done.6) | copy-start | bytes 2654212
  123.7 21.1 %copy-start.8 = (bf16[768,768]{1,0:T(8,128)(2,1)S(1)}, bf16[768,768]{1,0:T(8,128)(2,1)}, u32[]{:S(2)}) copy-start(bf16[768,768]{1,0:T(8,128)(2,1)} %constant.149.clone.low_source) | copy-start | bytes 3538948
  123.7 21.1 %copy-start.9 = (bf16[768,768]{1,0:T(8,128)(2,1)S(1)}, bf16[768,768]{1,0:T(8,128)(2,1)}, u32[]{:S(2)}) copy-start(bf16[768,768]{1,0:T(8,128)(2,1)} %constant.148.clone.high_source) | copy-start | bytes 3538948
  123.7 21.1 %copy-start.18 = (f32[12,384]{1,0:T(8,128)S(1)}, f32[12,384]{1,0:T(8,128)}, u32[]{:S(2)}) copy-start(f32[12,384]{1,0:T(8,128)} %constant.144.clone.sin_ref) | copy-start | bytes 55300
  123.7 21.1 %copy-start.21 = (f32[12,384]{1,0:T(8,128)S(1)}, f32[12,384]{1,0:T(8,128)}, u32[]{:S(2)}) copy-start(f32[12,384]{1,0:T(8,128)} %constant.143.clone.cos_ref) | copy-start | bytes 55300
  139.6 28.7 %all-to-all-start.1 = ((f32[8,48,1152]{2,1,0:T(8,128)}), f32[8,48,1152]{2,1,0:T(8,128)}, u32[]{:S(2)}, u32[]{:S(2)}) async-start(f32[8,48,1152]{2,1,0:T(8,128)} %shard_map.116), calls=%async_computation.1 | async-start | bytes 3538944 | tf_op jit(solution)/shard_map/all_to_all | solution.py:508
  144.8 1.2 copy-start.27
  152.1 1.9 collective-permute-start.11
  154.1 4.7 %collective-permute-start.14 = (f32[24,576]{1,0:T(8,128)S(1)}, f32[24,576]{1,0:T(8,128)S(1)}, u32[]{:S(2)}, u32[]{:S(2)}) collective-permute-start(f32[24,576]{1,0:T(8,128)S(1)} %select_select_fusion.14), channel_id=1, source_target_pairs={{0,48},{16,32},{32,16},{48,0},{64,112},{80,96},{96,80},{112,64},{1... | collective-permute-start | bytes 165896 | tf_op jit(solution)/shard_map/ppermute | solution.py:48
  155.9 11.1 %collective-permute-start.12 = (f32[24,576]{1,0:T(8,128)S(1)}, f32[24,576]{1,0:T(8,128)S(1)}, u32[]{:S(2)}, u32[]{:S(2)}) collective-permute-start(f32[24,576]{1,0:T(8,128)S(1)} %get-tuple-element.52), channel_id=1, source_target_pairs={{0,16},{16,0},{32,48},{48,32},{64,80},{80,64},{96,112},{112,96},{1... | collective-permute-start | bytes 165896 | tf_op jit(solution)/shard_map/ppermute | solution.py:48
  157.5 9.5 %collective-permute-start.13 = (f32[24,576]{1,0:T(8,128)S(1)}, f32[24,576]{1,0:T(8,128)S(1)}, u32[]{:S(2)}, u32[]{:S(2)}) collective-permute-start(f32[24,576]{1,0:T(8,128)S(1)} %get-tuple-element.53), channel_id=1, source_target_pairs={{0,32},{16,48},{32,0},{48,16},{64,96},{80,112},{96,64},{112,80},{1... | collective-permute-start | bytes 165896 | tf_op jit(solution)/shard_map/ppermute | solution.py:48
  176.9 10.2 %copy-start.28 = (f32[24,576]{1,0:T(8,128)S(1)}, f32[24,576]{1,0:T(8,128)}, u32[]{:S(2)}) copy-start(f32[24,576]{1,0:T(8,128)} %add_add_fusion.4) | copy-start | bytes 165892
  176.9 3.5 %collective-permute-start.15 = (f32[24,2304]{1,0:T(8,128)S(1)}, f32[24,2304]{1,0:T(8,128)S(1)}, u32[]{:S(2)}, u32[]{:S(2)}) collective-permute-start(f32[24,2304]{1,0:T(8,128)S(1)} %get-tuple-element.39), channel_id=1, source_target_pairs={{0,8},{8,0},{1,9},{9,1},{2,10},{10,2},{3,11},{11,3},{4,12},{12,4},... | collective-permute-start | bytes 663560 | tf_op jit(solution)/shard_map/ppermute | solution.py:38
  180.7 4.1 %collective-permute-start.18 = (f32[24,576]{1,0:T(8,128)S(1)}, f32[24,576]{1,0:T(8,128)S(1)}, u32[]{:S(2)}, u32[]{:S(2)}) collective-permute-start(f32[24,576]{1,0:T(8,128)S(1)} %select_select_fusion.11), channel_id=1, source_target_pairs={{0,48},{16,32},{32,16},{48,0},{64,112},{80,96},{96,80},{112,64},{1... | collective-permute-start | bytes 165896 | tf_op jit(solution)/shard_map/ppermute | solution.py:48
  182.2 4.5 %collective-permute-start.16 = (f32[24,576]{1,0:T(8,128)S(1)}, f32[24,576]{1,0:T(8,128)S(1)}, u32[]{:S(2)}, u32[]{:S(2)}) collective-permute-start(f32[24,576]{1,0:T(8,128)S(1)} %get-tuple-element.50), channel_id=1, source_target_pairs={{0,16},{16,0},{32,48},{48,32},{64,80},{80,64},{96,112},{112,96},{1... | collective-permute-start | bytes 165896 | tf_op jit(solution)/shard_map/ppermute | solution.py:48
  183.7 3.3 %collective-permute-start.17 = (f32[24,576]{1,0:T(8,128)S(1)}, f32[24,576]{1,0:T(8,128)S(1)}, u32[]{:S(2)}, u32[]{:S(2)}) collective-permute-start(f32[24,576]{1,0:T(8,128)S(1)} %get-tuple-element.51), channel_id=1, source_target_pairs={{0,32},{16,48},{32,0},{48,16},{64,96},{80,112},{96,64},{112,80},{1... | collective-permute-start | bytes 165896 | tf_op jit(solution)/shard_map/ppermute | solution.py:48
  187.2 6.5 %collective-permute-start.20 = (f32[48,576]{1,0:T(8,128)S(1)}, f32[48,576]{1,0:T(8,128)S(1)}, u32[]{:S(2)}, u32[]{:S(2)}) collective-permute-start(f32[48,576]{1,0:T(8,128)S(1)} %pad_maximum_fusion), channel_id=1, source_target_pairs={{0,64},{32,96},{64,128},{96,160},{128,192},{160,224},{192,0},{224,... | collective-permute-start | bytes 331784 | tf_op jit(solution)/shard_map/ppermute | solution.py:53
  189.0 4.9 %collective-permute-start.21 = (f32[48,576]{1,0:T(8,128)S(1)}, f32[48,576]{1,0:T(8,128)S(1)}, u32[]{:S(2)}, u32[]{:S(2)}) collective-permute-start(f32[48,576]{1,0:T(8,128)S(1)} %pad_maximum_fusion), channel_id=1, source_target_pairs={{0,192},{32,224},{64,0},{96,32},{128,64},{160,96},{192,128},{224,1... | collective-permute-start | bytes 331784 | tf_op jit(solution)/shard_map/ppermute | solution.py:53
  190.8 10.2 %collective-permute-start.19 = (f32[48,576]{1,0:T(8,128)S(1)}, f32[48,576]{1,0:T(8,128)S(1)}, u32[]{:S(2)}, u32[]{:S(2)}) collective-permute-start(f32[48,576]{1,0:T(8,128)S(1)} %pad_maximum_fusion), channel_id=1, source_target_pairs={{0,128},{32,160},{64,192},{96,224},{128,0},{160,32},{192,64},{224,... | collective-permute-start | bytes 331784 | tf_op jit(solution)/shard_map/ppermute | solution.py:53
  201.0 6.4 %collective-permute-start.24 = (f32[48,576]{1,0:T(8,128)S(1)}, f32[48,576]{1,0:T(8,128)S(1)}, u32[]{:S(2)}, u32[]{:S(2)}) collective-permute-start(f32[48,576]{1,0:T(8,128)S(1)} %add_add_fusion), channel_id=1, source_target_pairs={{0,48},{16,32},{32,16},{48,0},{64,112},{80,96},{96,80},{112,64},{1... | collective-permute-start | bytes 331784 | tf_op jit(solution)/shard_map/ppermute | solution.py:48
  205.2 4.7 %collective-permute-start.23 = (f32[48,576]{1,0:T(8,128)S(1)}, f32[48,576]{1,0:T(8,128)S(1)}, u32[]{:S(2)}, u32[]{:S(2)}) collective-permute-start(f32[48,576]{1,0:T(8,128)S(1)} %add_add_fusion), channel_id=1, source_target_pairs={{0,32},{16,48},{32,0},{48,16},{64,96},{80,112},{96,64},{112,80},{1... | collective-permute-start | bytes 331784 | tf_op jit(solution)/shard_map/ppermute | solution.py:48
  205.2 5.3 %collective-permute-start.22 = (f32[48,576]{1,0:T(8,128)S(1)}, f32[48,576]{1,0:T(8,128)S(1)}, u32[]{:S(2)}, u32[]{:S(2)}) collective-permute-start(f32[48,576]{1,0:T(8,128)S(1)} %add_add_fusion), channel_id=1, source_target_pairs={{0,16},{16,0},{32,48},{48,32},{64,80},{80,64},{96,112},{112,96},{1... | collective-permute-start | bytes 331784 | tf_op jit(solution)/shard_map/ppermute | solution.py:48
  210.7 3.2 %collective-permute-start.25 = (f32[48,2304]{1,0:T(8,128)S(1)}, f32[48,2304]{1,0:T(8,128)S(1)}, u32[]{:S(2)}, u32[]{:S(2)}) collective-permute-start(f32[48,2304]{1,0:T(8,128)S(1)} %concatenate.11.own_ref), channel_id=1, source_target_pairs={{0,8},{8,0},{1,9},{9,1},{2,10},{10,2},{3,11},{11,3},{4,12},{12,4},... | collective-permute-start | bytes 1327112 | tf_op jit(solution)/shard_map/ppermute | solution.py:38
  (11 other events, 9.9 us)
